TPU v7x, 128 devices: a whole 4x4x4 slice. The times are simulated.
128 devices in a mesh: seq: 16 (over x, z_hi, core), tp: 8 (over z_lo, y).
Axes of the slice: x: 4, y: 4, z: 4 (z_hi: 2, z_lo: 2; z = z_hi * 2 + z_lo), core: 2. Of those that a mesh axis runs over, the one named last changes fastest.
Arguments:
- queries: bfloat16 [8192, 64, 128], P('seq', 'tp'), may hold values from -8 to 8
- key_heads: bfloat16 [8192, 8, 128], P('seq', 'tp'), may hold values from -8 to 8
- value_heads: bfloat16 [8192, 8, 128], P('seq', 'tp'), may hold values from -16 to 16
- out_weight: bfloat16 [8192, 5120], P('tp'), may hold values from -0.0625 to 0.0625
- doc_lengths: int32 [4], replicated, may hold values from 1 to 4096, 8192 in all
- piece_owner: int32 [256], replicated, may hold values from 0 to 15, as said below
Outputs:
- mixed: bfloat16 [8192, 5120], P('seq', 'tp')
Inputs may be any that keep to these rules, and one draw needn't show every extreme that they name: Piece p of piece_owner covers tokens p * 32 to (p + 1) * 32 - 1. Every owner receives exactly 16 pieces, and at most 2 pieces come from the 16 pieces of one device to one owner. `doc_lengths`: the documents fill all 8192 tokens; the longest holds half of 8192.
All inputs are finite; a program needn't handle non-finite values.
Results may differ from a plain program's by a relative error of at most 0.019.
Values may be sent and summed in bfloat16 or wider, within the bound.
A program may use at most 64 MiB of HBM per device.

v0:
```python
import jax
import jax.numpy as jnp
from jax import lax
from jax.sharding import PartitionSpec as P

MASKED = -1e30


def shifted(value, axis, steps):
    count = lax.axis_size(axis)
    pairs = [(source, (source + steps) % count) for source in range(count)]
    return lax.ppermute(value, axis, pairs)


def doc_starts(doc_lengths, positions):
    doc_ends = jnp.cumsum(doc_lengths)
    ended = doc_ends[None, :] <= positions[:, None]
    return jnp.sum(jnp.where(ended, doc_lengths[None, :], 0), axis=1)


def outgoing(piece_owner, device, pieces, seq_count):
    local_owner = lax.dynamic_slice_in_dim(piece_owner, device * pieces, pieces)
    local_order = jnp.arange(pieces, dtype=jnp.int32)
    earlier = (local_owner[None, :] == local_owner[:, None]) & (
        local_order[None, :] < local_order[:, None]
    )
    slot_rank = jnp.sum(earlier.astype(jnp.int32), axis=1)
    target_slot = jnp.arange(seq_count * 2, dtype=jnp.int32)
    select = local_owner[None, :] * 2 + slot_rank[None, :] == target_slot[:, None]
    return select.astype(jnp.bfloat16)


def incoming(piece_owner, device, pieces):
    piece_total = piece_owner.shape[0]
    piece_ids = jnp.arange(piece_total, dtype=jnp.int32)
    is_mine = piece_owner == device
    mine_rank = jnp.cumsum(is_mine.astype(jnp.int32)) - 1
    my_slots = jnp.arange(pieces, dtype=jnp.int32)
    chosen = is_mine[None, :] & (mine_rank[None, :] == my_slots[:, None])
    held_pieces = jnp.sum(jnp.where(chosen, piece_ids[None, :], 0), axis=1)
    source_dev = held_pieces // pieces
    earlier_mine = (
        is_mine[None, :]
        & (piece_ids[None, :] // pieces == source_dev[:, None])
        & (piece_ids[None, :] < held_pieces[:, None])
    )
    slot_rank = jnp.sum(earlier_mine.astype(jnp.int32), axis=1)
    return (held_pieces, source_dev * 2 + slot_rank)


def route(row_data, select, arrival_slot, mover):
    pieces = select.shape[1]
    row_width = row_data.shape[1]
    piece_len = row_data.shape[0] // pieces
    stacked = row_data.reshape(pieces, piece_len * row_width)
    outgoing_rows = jnp.dot(select, stacked, preferred_element_type=jnp.float32).astype(
        row_data.dtype
    )
    arrived = mover(outgoing_rows.reshape(select.shape[0] * piece_len, row_width))
    arrived = arrived.reshape(select.shape[0], piece_len, row_width)
    return jnp.take(arrived, arrival_slot, axis=0).reshape(pieces * piece_len, row_width)


def attend(soft_state, grouped, kv_blocks, key_pos, query_pos, query_start, score_scale):
    run_max, run_sum, run_acc = soft_state
    key_block, value_block = kv_blocks
    scores = (
        jnp.einsum("qagd,kad->agqk", grouped, key_block, preferred_element_type=jnp.float32)
        * score_scale
    )
    visible = (key_pos[None, :] >= query_start[:, None]) & (key_pos[None, :] <= query_pos[:, None])
    scores = jnp.where(visible, scores, MASKED)
    new_max = jnp.maximum(run_max, jnp.max(scores, axis=-1))
    weights = jnp.where(visible, jnp.exp(scores - new_max[..., None]), 0.0)
    factor = jnp.exp(run_max - new_max)
    run_sum = run_sum * factor + jnp.sum(weights, axis=-1)
    update = jnp.einsum(
        "agqk,kad->agqd",
        weights.astype(jnp.bfloat16),
        value_block,
        preferred_element_type=jnp.float32,
    )
    run_acc = run_acc * factor[..., None] + update
    return (new_max, run_sum, run_acc)


def on_device(queries, key_heads, value_heads, out_weight, doc_lengths, piece_owner):
    seq_count = lax.axis_size("seq")
    device = lax.axis_index("seq")
    tok_rows = queries.shape[0]
    local_heads = queries.shape[1]
    head_dim = queries.shape[2]
    local_groups = key_heads.shape[1]
    per_group = local_heads // local_groups
    piece_len = tok_rows // seq_count
    score_scale = head_dim ** (-0.5)
    select = outgoing(piece_owner, device, seq_count, seq_count)
    held_pieces, arrival_slot = incoming(piece_owner, device, seq_count)
    offsets = jnp.arange(tok_rows, dtype=jnp.int32)

    def send_queries(buffer):
        return lax.all_to_all(buffer, "seq", split_axis=0, concat_axis=0, tiled=True)

    flat_rows = route(
        queries.reshape(tok_rows, local_heads * head_dim), select, arrival_slot, send_queries
    )
    query_rows = flat_rows.reshape(tok_rows, local_heads, head_dim)
    query_pos = (
        held_pieces[:, None] * piece_len + jnp.arange(piece_len, dtype=jnp.int32)[None, :]
    ).reshape(tok_rows)

    def pass_on(kv_blocks):
        return shifted((kv_blocks[0], kv_blocks[1]), "seq", 1)

    hop_count = seq_count - 1
    grouped = query_rows.reshape(tok_rows, local_groups, per_group, head_dim)
    query_start = doc_starts(doc_lengths, query_pos)
    start_max = jnp.full((local_groups, per_group, tok_rows), MASKED, jnp.float32)
    zero_sums = jnp.zeros((local_groups, per_group, tok_rows), jnp.float32)
    zero_acc = jnp.zeros((local_groups, per_group, tok_rows, head_dim), jnp.float32)
    kv_blocks = (key_heads, value_heads)
    soft_state = attend(
        (start_max, zero_sums, zero_acc),
        grouped,
        kv_blocks,
        device * tok_rows + offsets,
        query_pos,
        query_start,
        score_scale,
    )

    def one_hop(hop_index, hop_carry):
        held_blocks, held_state = hop_carry
        held_blocks = pass_on(held_blocks)
        source_dev = device - hop_index
        source_dev = jnp.mod(source_dev, seq_count)
        key_pos = source_dev * tok_rows + offsets
        return (
            held_blocks,
            attend(held_state, grouped, held_blocks, key_pos, query_pos, query_start, score_scale),
        )

    kv_blocks, soft_state = lax.fori_loop(1, hop_count + 1, one_hop, (kv_blocks, soft_state))
    run_max, run_sum, run_acc = soft_state
    attended = (run_acc / run_sum[..., None]).astype(jnp.bfloat16)
    attended = jnp.transpose(attended, (2, 0, 1, 3)).reshape(tok_rows, local_heads * head_dim)
    partial_sum = jnp.dot(attended, out_weight, preferred_element_type=jnp.float32)
    summed = lax.psum_scatter(
        partial_sum.astype(jnp.bfloat16), "tp", scatter_dimension=1, tiled=True
    )
    return summed


def solution(mesh):
    placed = (
        P("seq", "tp", None),
        P("seq", "tp", None),
        P("seq", "tp", None),
        P("tp", None),
        P(),
        P(),
    )
    return jax.shard_map(
        on_device, mesh=mesh, in_specs=placed, out_specs=P("seq", "tp"), check_vma=False
    )
```

profile of v0, /device:TPU:1, one launch (start us, length us, event | category | flops | bytes accessed | tf_op | source)
XLA Modules:
  0.0 398.7 jit_solution(6267331055575959160)
XLA Ops:
  7.5 1.6 copy.55
  10.7 1.5 reshape_reshape.3
  12.9 2.4 all_to_all.6
  15.3 9.1 %all-to-all-start = ((bf16[16,64,1024]{2,1,0:T(8,128)(2,1)}), bf16[16,64,1024]{2,1,0:T(8,128)(2,1)S(1)}, u32[]{:S(2)}, u32[]{:S(2)}) async-start(bf16[16,64,1024]{2,1,0:T(8,128)(2,1)} %all_to_all.6), calls=%async_computation | async-start | bytes 4194304 | tf_op jit(solution)/shard_map/all_to_all | solution.py:102
  26.9 26.0 %all-to-all-done = bf16[16,64,1024]{2,1,0:T(8,128)(2,1)S(1)} async-done(((bf16[16,64,1024]{2,1,0:T(8,128)(2,1)}), bf16[16,64,1024]{2,1,0:T(8,128)(2,1)S(1)}, u32[]{:S(2)}, u32[]{:S(2)}) %all-to-all-start) | async-done | bytes 2097184 | tf_op jit(solution)/shard_map/all_to_all | solution.py:102
  54.6 1.9 fusion.21
  56.6 2.0 fusion.23
  59.0 1.8 bitcast_select_fusion.2
  60.9 3.9 add_bitcast_fusion
  64.8 236.3 %while.24 = (s32[]{:T(128)}, bf16[512,1,128]{2,0,1:T(8,128)(2,1)S(1)}, bf16[512,1,128]{2,0,1:T(8,128)(2,1)S(1)}, f32[1,8,512]{2,1,0:T(8,128)S(1)}, f32[1,8,512]{...) while((s32[]{:T(128)}, ...), condition=%wide.region_12.13_spmd.clone, body=%wide.region_9.12_spmd.clone.sunk | while | flops 1102853120 | bytes 50346460 | solution.py:143
  64.8 3.2 collective-permute-start
  71.5 2.0 fusion.55
  73.6 3.1 bitcast_add_fusion.7
  78.1 4.0 collective-permute-start
  85.5 2.0 fusion.55
  87.7 3.1 bitcast_add_fusion.7
  92.2 4.0 collective-permute-start
  96.6 2.3 collective-permute-done
  100.4 2.0 fusion.55
  102.5 3.1 bitcast_add_fusion.7
  107.0 3.1 collective-permute-start
  110.7 4.4 %collective-permute-done = bf16[512,1,128]{2,0,1:T(8,128)(2,1)S(1)} collective-permute-done((bf16[512,1,128]{2,0,1:T(8,128)(2,1)S(1)}, bf16[512,1,128]{2,0,1:T(8,128)(2,1)S(1)}, u32[]{:S(2)}, u32[]{:S(2)}) %collective-permute-start) | collective-permute-done | bytes 131104 | tf_op jit(solution)/shard_map/while/body/eval_jaxpr/ppermute | solution.py:12
  115.1 1.5 fusion.53
  116.6 2.0 fusion.55
  118.7 3.1 bitcast_add_fusion.7
  124.7 6.5 %collective-permute-done = bf16[512,1,128]{2,0,1:T(8,128)(2,1)S(1)} collective-permute-done((bf16[512,1,128]{2,0,1:T(8,128)(2,1)S(1)}, bf16[512,1,128]{2,0,1:T(8,128)(2,1)S(1)}, u32[]{:S(2)}, u32[]{:S(2)}) %collective-permute-start) | collective-permute-done | bytes 131104 | tf_op jit(solution)/shard_map/while/body/eval_jaxpr/ppermute | solution.py:12
  132.8 2.0 fusion.55
  134.9 3.1 bitcast_add_fusion.7
  139.8 7.6 %collective-permute-done = bf16[512,1,128]{2,0,1:T(8,128)(2,1)S(1)} collective-permute-done((bf16[512,1,128]{2,0,1:T(8,128)(2,1)S(1)}, bf16[512,1,128]{2,0,1:T(8,128)(2,1)S(1)}, u32[]{:S(2)}, u32[]{:S(2)}) %collective-permute-start) | collective-permute-done | bytes 131104 | tf_op jit(solution)/shard_map/while/body/eval_jaxpr/ppermute | solution.py:12
  148.9 2.0 fusion.55
  151.1 3.1 bitcast_add_fusion.7
  156.0 7.6 %collective-permute-done = bf16[512,1,128]{2,0,1:T(8,128)(2,1)S(1)} collective-permute-done((bf16[512,1,128]{2,0,1:T(8,128)(2,1)S(1)}, bf16[512,1,128]{2,0,1:T(8,128)(2,1)S(1)}, u32[]{:S(2)}, u32[]{:S(2)}) %collective-permute-start) | collective-permute-done | bytes 131104 | tf_op jit(solution)/shard_map/while/body/eval_jaxpr/ppermute | solution.py:12
  165.1 2.0 fusion.55
  167.2 3.1 bitcast_add_fusion.7
  172.2 7.6 %collective-permute-done = bf16[512,1,128]{2,0,1:T(8,128)(2,1)S(1)} collective-permute-done((bf16[512,1,128]{2,0,1:T(8,128)(2,1)S(1)}, bf16[512,1,128]{2,0,1:T(8,128)(2,1)S(1)}, u32[]{:S(2)}, u32[]{:S(2)}) %collective-permute-start) | collective-permute-done | bytes 131104 | tf_op jit(solution)/shard_map/while/body/eval_jaxpr/ppermute | solution.py:12
  181.3 2.0 fusion.55
  183.4 3.1 bitcast_add_fusion.7
  188.4 7.6 %collective-permute-done = bf16[512,1,128]{2,0,1:T(8,128)(2,1)S(1)} collective-permute-done((bf16[512,1,128]{2,0,1:T(8,128)(2,1)S(1)}, bf16[512,1,128]{2,0,1:T(8,128)(2,1)S(1)}, u32[]{:S(2)}, u32[]{:S(2)}) %collective-permute-start) | collective-permute-done | bytes 131104 | tf_op jit(solution)/shard_map/while/body/eval_jaxpr/ppermute | solution.py:12
  197.5 2.0 fusion.55
  199.6 3.1 bitcast_add_fusion.7
  204.5 7.6 %collective-permute-done = bf16[512,1,128]{2,0,1:T(8,128)(2,1)S(1)} collective-permute-done((bf16[512,1,128]{2,0,1:T(8,128)(2,1)S(1)}, bf16[512,1,128]{2,0,1:T(8,128)(2,1)S(1)}, u32[]{:S(2)}, u32[]{:S(2)}) %collective-permute-start) | collective-permute-done | bytes 131104 | tf_op jit(solution)/shard_map/while/body/eval_jaxpr/ppermute | solution.py:12
  212.1 1.5 fusion.53
  213.6 2.0 fusion.55
  215.8 3.1 bitcast_add_fusion.7
  220.7 7.6 %collective-permute-done = bf16[512,1,128]{2,0,1:T(8,128)(2,1)S(1)} collective-permute-done((bf16[512,1,128]{2,0,1:T(8,128)(2,1)S(1)}, bf16[512,1,128]{2,0,1:T(8,128)(2,1)S(1)}, u32[]{:S(2)}, u32[]{:S(2)}) %collective-permute-start) | collective-permute-done | bytes 131104 | tf_op jit(solution)/shard_map/while/body/eval_jaxpr/ppermute | solution.py:12
  229.8 2.0 fusion.55
  231.9 3.1 bitcast_add_fusion.7
  236.9 7.6 %collective-permute-done = bf16[512,1,128]{2,0,1:T(8,128)(2,1)S(1)} collective-permute-done((bf16[512,1,128]{2,0,1:T(8,128)(2,1)S(1)}, bf16[512,1,128]{2,0,1:T(8,128)(2,1)S(1)}, u32[]{:S(2)}, u32[]{:S(2)}) %collective-permute-start) | collective-permute-done | bytes 131104 | tf_op jit(solution)/shard_map/while/body/eval_jaxpr/ppermute | solution.py:12
  246.0 2.0 fusion.55
  248.1 3.1 bitcast_add_fusion.7
  253.1 7.6 %collective-permute-done = bf16[512,1,128]{2,0,1:T(8,128)(2,1)S(1)} collective-permute-done((bf16[512,1,128]{2,0,1:T(8,128)(2,1)S(1)}, bf16[512,1,128]{2,0,1:T(8,128)(2,1)S(1)}, u32[]{:S(2)}, u32[]{:S(2)}) %collective-permute-start) | collective-permute-done | bytes 131104 | tf_op jit(solution)/shard_map/while/body/eval_jaxpr/ppermute | solution.py:12
  262.1 2.0 fusion.55
  264.3 3.1 bitcast_add_fusion.7
  269.2 7.6 %collective-permute-done = bf16[512,1,128]{2,0,1:T(8,128)(2,1)S(1)} collective-permute-done((bf16[512,1,128]{2,0,1:T(8,128)(2,1)S(1)}, bf16[512,1,128]{2,0,1:T(8,128)(2,1)S(1)}, u32[]{:S(2)}, u32[]{:S(2)}) %collective-permute-start) | collective-permute-done | bytes 131104 | tf_op jit(solution)/shard_map/while/body/eval_jaxpr/ppermute | solution.py:12
  278.3 2.0 fusion.55
  280.4 3.1 bitcast_add_fusion.7
  285.4 7.6 %collective-permute-done = bf16[512,1,128]{2,0,1:T(8,128)(2,1)S(1)} collective-permute-done((bf16[512,1,128]{2,0,1:T(8,128)(2,1)S(1)}, bf16[512,1,128]{2,0,1:T(8,128)(2,1)S(1)}, u32[]{:S(2)}, u32[]{:S(2)}) %collective-permute-start) | collective-permute-done | bytes 131104 | tf_op jit(solution)/shard_map/while/body/eval_jaxpr/ppermute | solution.py:12
  294.5 2.0 fusion.55
  296.6 3.1 bitcast_add_fusion.7
  301.1 1.9 copy.23
  303.3 11.6 %convolution_convert_fusion.1 = bf16[512,5120]{1,0:T(8,128)(2,1)} fusion(bf16[512,1024]{0,1:T(8,128)(2,1)S(1)} %bitcast.158, bf16[1024,5120]{1,0:T(8,128)(2,1)} %param.11), kind=kOutput, calls=%fused_computation.29 | convolution fusion | flops 5371330560 | bytes 16777216 | tf_op jit(solution)/shard_map/dot_general | solution.py:147
  315.0 7.9 %copy.26 = bf16[512,5120]{0,1:T(8,128)(2,1)} copy(bf16[512,5120]{1,0:T(8,128)(2,1)} %convolution_convert_fusion.1) | data formatting | bytes 10485760
  323.0 66.7 %reduce-scatter.4.cloned.1.call-done = bf16[640,512]{1,0:T(8,128)(2,1)} async-done(((bf16[5120,512]{1,0:T(8,128)(2,1)}), bf16[640,512]{1,0:T(8,128)(2,1)}) %reduce-scatter.4.cloned.1.call-update) | async-done | bytes 655376
  389.6 2.2 copy.27
  (305 shorter events, 59.3 us)
Async XLA Ops:
  6.5 18.9 %copy-start.10 = (s32[4]{0:T(128)S(1)}, s32[4]{0:T(128)}, u32[]{:S(2)}) copy-start(s32[4]{0:T(128)} %param.12) | copy-start | bytes 52
  6.5 18.0 %copy-start.7 = (s32[256]{0:T(256)S(1)}, s32[256]{0:T(256)}, u32[]{:S(2)}) copy-start(s32[256]{0:T(256)} %param.13) | copy-start | bytes 3076
  15.3 37.6 %all-to-all-start = ((bf16[16,64,1024]{2,1,0:T(8,128)(2,1)}), bf16[16,64,1024]{2,1,0:T(8,128)(2,1)S(1)}, u32[]{:S(2)}, u32[]{:S(2)}) async-start(bf16[16,64,1024]{2,1,0:T(8,128)(2,1)} %all_to_all.6), calls=%async_computation | async-start | bytes 4194304 | tf_op jit(solution)/shard_map/all_to_all | solution.py:102
  24.4 365.2 %reduce-scatter.4.cloned.1.call-start = ((), (), s32[]{:S(2)}) async-start(), calls=%async_computation.2 | async-start | bytes 5898240
  26.6 30.0 %copy-start.3 = (s32[512]{0:T(512)}, s32[512]{0:T(512)S(1)}, u32[]{:S(2)}) copy-start(s32[512]{0:T(512)S(1)} %select_reduce_fusion.1) | copy-start | bytes 6148
  54.6 4.3 %copy-start.8 = (pred[512]{0:T(512)(128)(4,1)S(1)}, pred[512]{0:T(512)(128)(4,1)}, u32[]{:S(2)}) copy-start(pred[512]{0:T(512)(128)(4,1)} %broadcast_in_dim.152) | copy-start | bytes 1540
  56.6 4.3 %copy-start.2 = (bf16[512,1,128]{2,0,1:T(8,128)(2,1)S(1)}, bf16[512,1,128]{2,0,1:T(8,128)(2,1)}, u32[]{:S(2)}) copy-start(bf16[512,1,128]{2,0,1:T(8,128)(2,1)} %copy.55) | copy-start | bytes 393220
  60.9 4.0 copy-start.4
  60.9 3.9 copy-start.6
  64.8 5.1 %collective-permute-start = (bf16[512,1,128]{2,0,1:T(8,128)(2,1)S(1)}, bf16[512,1,128]{2,0,1:T(8,128)(2,1)S(1)}, u32[]{:S(2)}, u32[]{:S(2)}) collective-permute-start(bf16[512,1,128]{2,0,1:T(8,128)(2,1)S(1)} %get-tuple-element.445), channel_id=1, source_target_pairs={{0,8},{8,16},{16,24},{24,32},{32,40},{40,48},{48,56},{56,64},{64,7... | collective-permute-start | bytes 393224 | tf_op jit(solution)/shard_map/while/body/eval_jaxpr/ppermute | solution.py:12
  68.0 5.6 %collective-permute-start.1 = (bf16[512,1,128]{2,0,1:T(8,128)(2,1)S(1)}, bf16[512,1,128]{2,0,1:T(8,128)(2,1)S(1)}, u32[]{:S(2)}, u32[]{:S(2)}) collective-permute-start(bf16[512,1,128]{2,0,1:T(8,128)(2,1)S(1)} %get-tuple-element.446), channel_id=1, source_target_pairs={{0,8},{8,16},{16,24},{24,32},{32,40},{40,48},{48,56},{56,64},{64,7... | collective-permute-start | bytes 393224 | tf_op jit(solution)/shard_map/while/body/eval_jaxpr/ppermute | solution.py:12
  70.0 3.7 copy-start
  76.8 1.4 copy-start.1
  78.1 5.9 %collective-permute-start = (bf16[512,1,128]{2,0,1:T(8,128)(2,1)S(1)}, bf16[512,1,128]{2,0,1:T(8,128)(2,1)S(1)}, u32[]{:S(2)}, u32[]{:S(2)}) collective-permute-start(bf16[512,1,128]{2,0,1:T(8,128)(2,1)S(1)} %get-tuple-element.445), channel_id=1, source_target_pairs={{0,8},{8,16},{16,24},{24,32},{32,40},{40,48},{48,56},{56,64},{64,7... | collective-permute-start | bytes 393224 | tf_op jit(solution)/shard_map/while/body/eval_jaxpr/ppermute | solution.py:12
  82.1 5.6 %collective-permute-start.1 = (bf16[512,1,128]{2,0,1:T(8,128)(2,1)S(1)}, bf16[512,1,128]{2,0,1:T(8,128)(2,1)S(1)}, u32[]{:S(2)}, u32[]{:S(2)}) collective-permute-start(bf16[512,1,128]{2,0,1:T(8,128)(2,1)S(1)} %get-tuple-element.446), channel_id=1, source_target_pairs={{0,8},{8,16},{16,24},{24,32},{32,40},{40,48},{48,56},{56,64},{64,7... | collective-permute-start | bytes 393224 | tf_op jit(solution)/shard_map/while/body/eval_jaxpr/ppermute | solution.py:12
  84.0 3.6 copy-start
  90.8 1.4 copy-start.1
  92.2 6.7 %collective-permute-start = (bf16[512,1,128]{2,0,1:T(8,128)(2,1)S(1)}, bf16[512,1,128]{2,0,1:T(8,128)(2,1)S(1)}, u32[]{:S(2)}, u32[]{:S(2)}) collective-permute-start(bf16[512,1,128]{2,0,1:T(8,128)(2,1)S(1)} %get-tuple-element.445), channel_id=1, source_target_pairs={{0,8},{8,16},{16,24},{24,32},{32,40},{40,48},{48,56},{56,64},{64,7... | collective-permute-start | bytes 393224 | tf_op jit(solution)/shard_map/while/body/eval_jaxpr/ppermute | solution.py:12
  96.1 6.4 %collective-permute-start.1 = (bf16[512,1,128]{2,0,1:T(8,128)(2,1)S(1)}, bf16[512,1,128]{2,0,1:T(8,128)(2,1)S(1)}, u32[]{:S(2)}, u32[]{:S(2)}) collective-permute-start(bf16[512,1,128]{2,0,1:T(8,128)(2,1)S(1)} %get-tuple-element.446), channel_id=1, source_target_pairs={{0,8},{8,16},{16,24},{24,32},{32,40},{40,48},{48,56},{56,64},{64,7... | collective-permute-start | bytes 393224 | tf_op jit(solution)/shard_map/while/body/eval_jaxpr/ppermute | solution.py:12
  98.9 3.7 copy-start
  105.7 1.4 copy-start.1
  107.0 8.0 %collective-permute-start = (bf16[512,1,128]{2,0,1:T(8,128)(2,1)S(1)}, bf16[512,1,128]{2,0,1:T(8,128)(2,1)S(1)}, u32[]{:S(2)}, u32[]{:S(2)}) collective-permute-start(bf16[512,1,128]{2,0,1:T(8,128)(2,1)S(1)} %get-tuple-element.445), channel_id=1, source_target_pairs={{0,8},{8,16},{16,24},{24,32},{32,40},{40,48},{48,56},{56,64},{64,7... | collective-permute-start | bytes 393224 | tf_op jit(solution)/shard_map/while/body/eval_jaxpr/ppermute | solution.py:12
  110.2 8.5 %collective-permute-start.1 = (bf16[512,1,128]{2,0,1:T(8,128)(2,1)S(1)}, bf16[512,1,128]{2,0,1:T(8,128)(2,1)S(1)}, u32[]{:S(2)}, u32[]{:S(2)}) collective-permute-start(bf16[512,1,128]{2,0,1:T(8,128)(2,1)S(1)} %get-tuple-element.446), channel_id=1, source_target_pairs={{0,8},{8,16},{16,24},{24,32},{32,40},{40,48},{48,56},{56,64},{64,7... | collective-permute-start | bytes 393224 | tf_op jit(solution)/shard_map/while/body/eval_jaxpr/ppermute | solution.py:12
  115.1 3.7 copy-start
  121.9 1.4 copy-start.1
  123.2 8.0 %collective-permute-start = (bf16[512,1,128]{2,0,1:T(8,128)(2,1)S(1)}, bf16[512,1,128]{2,0,1:T(8,128)(2,1)S(1)}, u32[]{:S(2)}, u32[]{:S(2)}) collective-permute-start(bf16[512,1,128]{2,0,1:T(8,128)(2,1)S(1)} %get-tuple-element.445), channel_id=1, source_target_pairs={{0,8},{8,16},{16,24},{24,32},{32,40},{40,48},{48,56},{56,64},{64,7... | collective-permute-start | bytes 393224 | tf_op jit(solution)/shard_map/while/body/eval_jaxpr/ppermute | solution.py:12
  124.3 10.6 %collective-permute-start.1 = (bf16[512,1,128]{2,0,1:T(8,128)(2,1)S(1)}, bf16[512,1,128]{2,0,1:T(8,128)(2,1)S(1)}, u32[]{:S(2)}, u32[]{:S(2)}) collective-permute-start(bf16[512,1,128]{2,0,1:T(8,128)(2,1)S(1)} %get-tuple-element.446), channel_id=1, source_target_pairs={{0,8},{8,16},{16,24},{24,32},{32,40},{40,48},{48,56},{56,64},{64,7... | collective-permute-start | bytes 393224 | tf_op jit(solution)/shard_map/while/body/eval_jaxpr/ppermute | solution.py:12
  131.2 3.7 copy-start
  138.0 1.4 copy-start.1
  139.4 8.0 %collective-permute-start = (bf16[512,1,128]{2,0,1:T(8,128)(2,1)S(1)}, bf16[512,1,128]{2,0,1:T(8,128)(2,1)S(1)}, u32[]{:S(2)}, u32[]{:S(2)}) collective-permute-start(bf16[512,1,128]{2,0,1:T(8,128)(2,1)S(1)} %get-tuple-element.445), channel_id=1, source_target_pairs={{0,8},{8,16},{16,24},{24,32},{32,40},{40,48},{48,56},{56,64},{64,7... | collective-permute-start | bytes 393224 | tf_op jit(solution)/shard_map/while/body/eval_jaxpr/ppermute | solution.py:12
  139.4 11.6 %collective-permute-start.1 = (bf16[512,1,128]{2,0,1:T(8,128)(2,1)S(1)}, bf16[512,1,128]{2,0,1:T(8,128)(2,1)S(1)}, u32[]{:S(2)}, u32[]{:S(2)}) collective-permute-start(bf16[512,1,128]{2,0,1:T(8,128)(2,1)S(1)} %get-tuple-element.446), channel_id=1, source_target_pairs={{0,8},{8,16},{16,24},{24,32},{32,40},{40,48},{48,56},{56,64},{64,7... | collective-permute-start | bytes 393224 | tf_op jit(solution)/shard_map/while/body/eval_jaxpr/ppermute | solution.py:12
  147.4 3.7 copy-start
  154.2 1.4 copy-start.1
  155.6 8.0 %collective-permute-start = (bf16[512,1,128]{2,0,1:T(8,128)(2,1)S(1)}, bf16[512,1,128]{2,0,1:T(8,128)(2,1)S(1)}, u32[]{:S(2)}, u32[]{:S(2)}) collective-permute-start(bf16[512,1,128]{2,0,1:T(8,128)(2,1)S(1)} %get-tuple-element.445), channel_id=1, source_target_pairs={{0,8},{8,16},{16,24},{24,32},{32,40},{40,48},{48,56},{56,64},{64,7... | collective-permute-start | bytes 393224 | tf_op jit(solution)/shard_map/while/body/eval_jaxpr/ppermute | solution.py:12
  155.6 11.6 %collective-permute-start.1 = (bf16[512,1,128]{2,0,1:T(8,128)(2,1)S(1)}, bf16[512,1,128]{2,0,1:T(8,128)(2,1)S(1)}, u32[]{:S(2)}, u32[]{:S(2)}) collective-permute-start(bf16[512,1,128]{2,0,1:T(8,128)(2,1)S(1)} %get-tuple-element.446), channel_id=1, source_target_pairs={{0,8},{8,16},{16,24},{24,32},{32,40},{40,48},{48,56},{56,64},{64,7... | collective-permute-start | bytes 393224 | tf_op jit(solution)/shard_map/while/body/eval_jaxpr/ppermute | solution.py:12
  163.6 3.7 copy-start
  170.4 1.4 copy-start.1
  171.7 8.0 %collective-permute-start = (bf16[512,1,128]{2,0,1:T(8,128)(2,1)S(1)}, bf16[512,1,128]{2,0,1:T(8,128)(2,1)S(1)}, u32[]{:S(2)}, u32[]{:S(2)}) collective-permute-start(bf16[512,1,128]{2,0,1:T(8,128)(2,1)S(1)} %get-tuple-element.445), channel_id=1, source_target_pairs={{0,8},{8,16},{16,24},{24,32},{32,40},{40,48},{48,56},{56,64},{64,7... | collective-permute-start | bytes 393224 | tf_op jit(solution)/shard_map/while/body/eval_jaxpr/ppermute | solution.py:12
  171.7 11.6 %collective-permute-start.1 = (bf16[512,1,128]{2,0,1:T(8,128)(2,1)S(1)}, bf16[512,1,128]{2,0,1:T(8,128)(2,1)S(1)}, u32[]{:S(2)}, u32[]{:S(2)}) collective-permute-start(bf16[512,1,128]{2,0,1:T(8,128)(2,1)S(1)} %get-tuple-element.446), channel_id=1, source_target_pairs={{0,8},{8,16},{16,24},{24,32},{32,40},{40,48},{48,56},{56,64},{64,7... | collective-permute-start | bytes 393224 | tf_op jit(solution)/shard_map/while/body/eval_jaxpr/ppermute | solution.py:12
  179.7 3.7 copy-start
  187.9 8.0 %collective-permute-start = (bf16[512,1,128]{2,0,1:T(8,128)(2,1)S(1)}, bf16[512,1,128]{2,0,1:T(8,128)(2,1)S(1)}, u32[]{:S(2)}, u32[]{:S(2)}) collective-permute-start(bf16[512,1,128]{2,0,1:T(8,128)(2,1)S(1)} %get-tuple-element.445), channel_id=1, source_target_pairs={{0,8},{8,16},{16,24},{24,32},{32,40},{40,48},{48,56},{56,64},{64,7... | collective-permute-start | bytes 393224 | tf_op jit(solution)/shard_map/while/body/eval_jaxpr/ppermute | solution.py:12
  187.9 11.6 %collective-permute-start.1 = (bf16[512,1,128]{2,0,1:T(8,128)(2,1)S(1)}, bf16[512,1,128]{2,0,1:T(8,128)(2,1)S(1)}, u32[]{:S(2)}, u32[]{:S(2)}) collective-permute-start(bf16[512,1,128]{2,0,1:T(8,128)(2,1)S(1)} %get-tuple-element.446), channel_id=1, source_target_pairs={{0,8},{8,16},{16,24},{24,32},{32,40},{40,48},{48,56},{56,64},{64,7... | collective-permute-start | bytes 393224 | tf_op jit(solution)/shard_map/while/body/eval_jaxpr/ppermute | solution.py:12
  195.9 3.7 copy-start
  204.1 8.0 %collective-permute-start = (bf16[512,1,128]{2,0,1:T(8,128)(2,1)S(1)}, bf16[512,1,128]{2,0,1:T(8,128)(2,1)S(1)}, u32[]{:S(2)}, u32[]{:S(2)}) collective-permute-start(bf16[512,1,128]{2,0,1:T(8,128)(2,1)S(1)} %get-tuple-element.445), channel_id=1, source_target_pairs={{0,8},{8,16},{16,24},{24,32},{32,40},{40,48},{48,56},{56,64},{64,7... | collective-permute-start | bytes 393224 | tf_op jit(solution)/shard_map/while/body/eval_jaxpr/ppermute | solution.py:12
  204.1 11.6 %collective-permute-start.1 = (bf16[512,1,128]{2,0,1:T(8,128)(2,1)S(1)}, bf16[512,1,128]{2,0,1:T(8,128)(2,1)S(1)}, u32[]{:S(2)}, u32[]{:S(2)}) collective-permute-start(bf16[512,1,128]{2,0,1:T(8,128)(2,1)S(1)} %get-tuple-element.446), channel_id=1, source_target_pairs={{0,8},{8,16},{16,24},{24,32},{32,40},{40,48},{48,56},{56,64},{64,7... | collective-permute-start | bytes 393224 | tf_op jit(solution)/shard_map/while/body/eval_jaxpr/ppermute | solution.py:12
  212.1 3.7 copy-start
  218.9 1.4 copy-start.1
  220.3 8.0 %collective-permute-start = (bf16[512,1,128]{2,0,1:T(8,128)(2,1)S(1)}, bf16[512,1,128]{2,0,1:T(8,128)(2,1)S(1)}, u32[]{:S(2)}, u32[]{:S(2)}) collective-permute-start(bf16[512,1,128]{2,0,1:T(8,128)(2,1)S(1)} %get-tuple-element.445), channel_id=1, source_target_pairs={{0,8},{8,16},{16,24},{24,32},{32,40},{40,48},{48,56},{56,64},{64,7... | collective-permute-start | bytes 393224 | tf_op jit(solution)/shard_map/while/body/eval_jaxpr/ppermute | solution.py:12
  220.3 11.6 %collective-permute-start.1 = (bf16[512,1,128]{2,0,1:T(8,128)(2,1)S(1)}, bf16[512,1,128]{2,0,1:T(8,128)(2,1)S(1)}, u32[]{:S(2)}, u32[]{:S(2)}) collective-permute-start(bf16[512,1,128]{2,0,1:T(8,128)(2,1)S(1)} %get-tuple-element.446), channel_id=1, source_target_pairs={{0,8},{8,16},{16,24},{24,32},{32,40},{40,48},{48,56},{56,64},{64,7... | collective-permute-start | bytes 393224 | tf_op jit(solution)/shard_map/while/body/eval_jaxpr/ppermute | solution.py:12
  228.3 3.7 copy-start
  236.4 8.0 %collective-permute-start = (bf16[512,1,128]{2,0,1:T(8,128)(2,1)S(1)}, bf16[512,1,128]{2,0,1:T(8,128)(2,1)S(1)}, u32[]{:S(2)}, u32[]{:S(2)}) collective-permute-start(bf16[512,1,128]{2,0,1:T(8,128)(2,1)S(1)} %get-tuple-element.445), channel_id=1, source_target_pairs={{0,8},{8,16},{16,24},{24,32},{32,40},{40,48},{48,56},{56,64},{64,7... | collective-permute-start | bytes 393224 | tf_op jit(solution)/shard_map/while/body/eval_jaxpr/ppermute | solution.py:12
  236.4 11.6 %collective-permute-start.1 = (bf16[512,1,128]{2,0,1:T(8,128)(2,1)S(1)}, bf16[512,1,128]{2,0,1:T(8,128)(2,1)S(1)}, u32[]{:S(2)}, u32[]{:S(2)}) collective-permute-start(bf16[512,1,128]{2,0,1:T(8,128)(2,1)S(1)} %get-tuple-element.446), channel_id=1, source_target_pairs={{0,8},{8,16},{16,24},{24,32},{32,40},{40,48},{48,56},{56,64},{64,7... | collective-permute-start | bytes 393224 | tf_op jit(solution)/shard_map/while/body/eval_jaxpr/ppermute | solution.py:12
  244.4 3.7 copy-start
  251.3 1.4 copy-start.1
  252.6 8.0 %collective-permute-start = (bf16[512,1,128]{2,0,1:T(8,128)(2,1)S(1)}, bf16[512,1,128]{2,0,1:T(8,128)(2,1)S(1)}, u32[]{:S(2)}, u32[]{:S(2)}) collective-permute-start(bf16[512,1,128]{2,0,1:T(8,128)(2,1)S(1)} %get-tuple-element.445), channel_id=1, source_target_pairs={{0,8},{8,16},{16,24},{24,32},{32,40},{40,48},{48,56},{56,64},{64,7... | collective-permute-start | bytes 393224 | tf_op jit(solution)/shard_map/while/body/eval_jaxpr/ppermute | solution.py:12
  252.6 11.6 %collective-permute-start.1 = (bf16[512,1,128]{2,0,1:T(8,128)(2,1)S(1)}, bf16[512,1,128]{2,0,1:T(8,128)(2,1)S(1)}, u32[]{:S(2)}, u32[]{:S(2)}) collective-permute-start(bf16[512,1,128]{2,0,1:T(8,128)(2,1)S(1)} %get-tuple-element.446), channel_id=1, source_target_pairs={{0,8},{8,16},{16,24},{24,32},{32,40},{40,48},{48,56},{56,64},{64,7... | collective-permute-start | bytes 393224 | tf_op jit(solution)/shard_map/while/body/eval_jaxpr/ppermute | solution.py:12
  260.6 3.7 copy-start
  268.8 8.0 %collective-permute-start = (bf16[512,1,128]{2,0,1:T(8,128)(2,1)S(1)}, bf16[512,1,128]{2,0,1:T(8,128)(2,1)S(1)}, u32[]{:S(2)}, u32[]{:S(2)}) collective-permute-start(bf16[512,1,128]{2,0,1:T(8,128)(2,1)S(1)} %get-tuple-element.445), channel_id=1, source_target_pairs={{0,8},{8,16},{16,24},{24,32},{32,40},{40,48},{48,56},{56,64},{64,7... | collective-permute-start | bytes 393224 | tf_op jit(solution)/shard_map/while/body/eval_jaxpr/ppermute | solution.py:12
  268.8 11.6 %collective-permute-start.1 = (bf16[512,1,128]{2,0,1:T(8,128)(2,1)S(1)}, bf16[512,1,128]{2,0,1:T(8,128)(2,1)S(1)}, u32[]{:S(2)}, u32[]{:S(2)}) collective-permute-start(bf16[512,1,128]{2,0,1:T(8,128)(2,1)S(1)} %get-tuple-element.446), channel_id=1, source_target_pairs={{0,8},{8,16},{16,24},{24,32},{32,40},{40,48},{48,56},{56,64},{64,7... | collective-permute-start | bytes 393224 | tf_op jit(solution)/shard_map/while/body/eval_jaxpr/ppermute | solution.py:12
  276.8 3.7 copy-start
  285.0 8.0 %collective-permute-start = (bf16[512,1,128]{2,0,1:T(8,128)(2,1)S(1)}, bf16[512,1,128]{2,0,1:T(8,128)(2,1)S(1)}, u32[]{:S(2)}, u32[]{:S(2)}) collective-permute-start(bf16[512,1,128]{2,0,1:T(8,128)(2,1)S(1)} %get-tuple-element.445), channel_id=1, source_target_pairs={{0,8},{8,16},{16,24},{24,32},{32,40},{40,48},{48,56},{56,64},{64,7... | collective-permute-start | bytes 393224 | tf_op jit(solution)/shard_map/while/body/eval_jaxpr/ppermute | solution.py:12
  285.0 11.6 %collective-permute-start.1 = (bf16[512,1,128]{2,0,1:T(8,128)(2,1)S(1)}, bf16[512,1,128]{2,0,1:T(8,128)(2,1)S(1)}, u32[]{:S(2)}, u32[]{:S(2)}) collective-permute-start(bf16[512,1,128]{2,0,1:T(8,128)(2,1)S(1)} %get-tuple-element.446), channel_id=1, source_target_pairs={{0,8},{8,16},{16,24},{24,32},{32,40},{40,48},{48,56},{56,64},{64,7... | collective-permute-start | bytes 393224 | tf_op jit(solution)/shard_map/while/body/eval_jaxpr/ppermute | solution.py:12
  293.0 3.7 copy-start
  299.8 1.4 copy-start.1
  (7 other events, 8.8 us)
Sparse Core Ops, SparseCore 0:
  323.1 66.5 reduce-scatter.3
where the time goes:
time: 399 us
  waiting for transfers between devices  184 us (46%)
  matrix products  87.9 us (22%)
  other arithmetic  43.3 us (11%)
  local copies, waits for them, and re-layouts  43.2 us (11%)
  starting transfers between devices  24.9 us (6%)
  between operations  13.6 us (3%)
    ppermute x30, waiting for transfers between devices, shifted(): return lax.ppermute(value, axis, pairs)  91.5 us
    unnamed x2, waiting for transfers between devices  66.7 us
    dot_general x16, matrix products, attend(): jnp.einsum('agqk,kad->agqd', weights.astype(jnp.bfloat16), value_block, p...  51.1 us
    reduce_sum x16, other arithmetic, attend(): run_sum = run_sum * factor + jnp.sum(weights, axis=-1)  32.5 us
    all_to_all x1, waiting for transfers between devices, send_queries(): lax.all_to_all(buffer, 'seq', split_axis=0, concat_axis=0, tiled=True)  26 us
    dot_general x16, matrix products, attend(): jnp.einsum('qagd,kad->agqk', grouped, key_block, preferred_element_type=j...  24.5 us
    while x105, local copies, waits for them, and re-layouts  20.6 us
    ppermute x30, starting transfers between devices, shifted(): return lax.ppermute(value, axis, pairs)  15.7 us
  transfers between devices with their start and end apart: 32, of which 17 were waited for; matrix products, arithmetic and copies ran while one was open for 16% of the time, Pallas kernels for 0%

commit v1 on v0

v1 whole, which is shorter than its diff:
```python
import functools

import jax
import jax.numpy as jnp
from jax import lax
from jax.experimental import pallas as pl
from jax.experimental.pallas import tpu as pltpu
from jax.sharding import PartitionSpec as P

MASKED = -1e30
BF16, F32, I32 = jnp.bfloat16, jnp.float32, jnp.int32
ROWS = 512
HEADS = 8
HD = 128
HALF = 256
GROUP = 3
SPAN = GROUP * ROWS
BACK = 8
SCORE = HD**-0.5 * 1.4426950408889634
MESH = pl.DeviceIdType.MESH


def places():
    s = lax.axis_index("seq")
    x, z, core = s // 4, (s // 2) % 2, s % 2

    def at(step, flip_z, flip_core):
        return ((x + step) % 4) * 4 + ((z + flip_z) % 2) * 2 + (core + flip_core) % 2

    return s, z, core, at


def slot(ref_k, ref_v, delta):
    g, r = delta // GROUP, delta % GROUP
    start = pl.multiple_of(r * ROWS, ROWS)
    return (
        ref_k.at[g, pl.ds(start, ROWS), pl.ds(0, HD)],
        ref_v.at[g, pl.ds(0, HD), pl.ds(start, ROWS)],
    )


def doc_of(ends, positions):
    doc = jnp.where(positions < 0, -1, 0)
    for end in ends:
        doc = doc + jnp.where(positions >= end, 1, 0)
    return doc


def attend_kernel(
    q_ref, k_ref, v_ref, len_ref, o_ref, qx, kx, vx, acc, top, diff, s0, s1, p0, p1, send, recv
):
    s, z, core, at = places()
    sibling, next_x, prev_x, far_x, other_z = (
        at(0, 0, 1),
        at(1, 0, 0),
        at(3, 0, 0),
        at(2, 0, 0),
        at(0, 1, 0),
    )
    barrier = pltpu.get_barrier_semaphore()
    for peer in (sibling, next_x, prev_x, far_x, other_z):
        pl.semaphore_signal(barrier, inc=1, device_id={"seq": peer}, device_id_type=MESH)

    kx[0, :ROWS, :HD] = k_ref[...]
    vx[0, :HD, :ROWS] = v_ref[...].T
    pl.semaphore_wait(barrier, 5)

    sends = []

    def copies(index, source, target, peer):
        for part, (a, b) in enumerate(zip(slot(kx, vx, source), slot(kx, vx, target))):
            yield pltpu.make_async_remote_copy(
                src_ref=a,
                dst_ref=b,
                send_sem=send.at[index, part],
                recv_sem=recv.at[target, part],
                device_id={"seq": peer},
                device_id_type=MESH,
            )

    def go(index, source, target, peer):
        for copy in copies(index, source, target, peer):
            copy.start()

    def arrived(target):
        for copy in copies(0, 0, target, sibling):
            copy.wait_recv()

    def to_sibling(i):
        go(4 + i, 2 * i + 2 * core, 2 * i + 1, sibling)

    def to_z(i):
        go(2 + i, 4 * z + 4 * i, 2 + 4 * i, other_z)

    go(0, 0, 4, next_x)

    @pl.when(z == 0)
    def _():
        to_z(0)

    @pl.when(core == 0)
    def _():
        to_sibling(0)

    go(1, 0, 8, far_x)

    ends = []
    total = 0
    for d in range(4):
        total = total + len_ref[d]
        ends.append(total)
    lane = lax.broadcasted_iota(I32, (ROWS, HD), 1)
    row = lax.broadcasted_iota(I32, (ROWS, HD), 0)
    mine = jnp.where(doc_of(ends, row + s * ROWS) == lane, MASKED, 0.0).astype(BF16)
    for h in range(HEADS):
        for half in range(2):
            rows = pl.ds(half * HALF, HALF)
            qx[half, h, :, :HD] = q_ref[rows, pl.ds(h * HD, HD)]
            qx[half, h, :, HD:] = mine[half * HALF : (half + 1) * HALF]

    def mark(delta, _):
        start = pl.multiple_of((delta % GROUP) * ROWS, ROWS)
        seen = doc_of(ends, row + (s - delta) * ROWS) == lane
        kx[delta // GROUP, pl.ds(start, ROWS), HD:] = jnp.where(seen, 0.0, 1.0).astype(BF16)
        return 0

    lax.fori_loop(0, BACK + 1, mark, 0)
    for g in range(GROUP):
        vx[g, HD:, :] = jnp.ones((16, SPAN), BF16)
    diff[...] = lax.broadcasted_iota(I32, (ROWS, HALF), 0) - lax.broadcasted_iota(
        I32, (ROWS, HALF), 1
    )
    acc[...] = jnp.zeros_like(acc)
    top[...] = jnp.full_like(top, MASKED)

    arrived(4)

    @pl.when(z == 1)
    def _():
        to_z(0)

    @pl.when(z == 0)
    def _():
        to_z(1)

    @pl.when(core == 0)
    def _():
        to_sibling(2)

    @pl.when(core == 1)
    def _():
        to_sibling(1)

    arrived(2)

    @pl.when(core == 0)
    def _():
        to_sibling(1)

    @pl.when(core == 1)
    def _():
        to_sibling(0)

    arrived(1)

    scores, weights = (s0, s1), (p0, p1)

    def matrix(a, b):
        return lax.dot_general(a, b, (((1,), (1,)), ((), ())), preferred_element_type=F32)

    def one_pass(step, _):
        @pl.when(step == 1)
        def _():
            arrived(8)

            @pl.when(z == 1)
            def _():
                to_z(1)

            @pl.when(core == 1)
            def _():
                to_sibling(3)

        @pl.when(step == 2)
        def _():
            arrived(6)

            @pl.when(core == 0)
            def _():
                to_sibling(3)

            @pl.when(core == 1)
            def _():
                to_sibling(2)

            arrived(3)
            arrived(5)

        @pl.when(step == 3)
        def _():
            arrived(7)

        g = jnp.where(step < 2, 0, 1 + step % 2)
        half = jnp.where(step < 2, step, (step - 2) // 2)
        limit = half * HALF + g * SPAN
        factor = {}
        for i in range(HEADS + 2):
            if i < HEADS:
                out = scores[i % 2]
                qh = qx[half, i]
                out[:ROWS] = jnp.where(
                    diff[...] <= limit, matrix(kx[g, :ROWS, :], qh), MASKED
                )
                out[ROWS:] = matrix(kx[g, ROWS:, :], qh)
            if 0 <= i - 1 < HEADS:
                h = i - 1
                sc = scores[h % 2][...]
                before = top[half, h, :1, :]
                now = jnp.maximum(before, jnp.max(sc, axis=0, keepdims=True))
                weights[h % 2][...] = jnp.exp2((sc - now) * SCORE).astype(BF16)
                factor[h] = jnp.exp2((before - now) * SCORE)
                top[half, h, :1, :] = now
            if 0 <= i - 2 < HEADS:
                h = i - 2
                acc[half, h] = acc[half, h] * factor[h] + jnp.dot(
                    vx[g], weights[h % 2][...], preferred_element_type=F32
                )
        return 0

    lax.fori_loop(0, 6, one_pass, 0)

    for half in range(2):
        for h in range(HEADS):
            value = acc[half, h, :HD, :] / acc[half, h, HD : HD + 1, :]
            o_ref[pl.ds(half * HALF, HALF), pl.ds(h * HD, HD)] = value.T.astype(BF16)

    for index in range(4):
        for copy in copies(index, 0, 1, sibling):
            copy.wait_send()
    for i in range(4):
        for copy in copies(4 + i, 0, 1, sibling):
            copy.wait_send()


def attention(queries, key_rows, value_rows, doc_lengths):
    vmem = pl.BlockSpec(memory_space=pltpu.VMEM)
    return pl.pallas_call(
        attend_kernel,
        out_shape=jax.ShapeDtypeStruct((ROWS, HEADS * HD), BF16),
        in_specs=[vmem, vmem, vmem, pl.BlockSpec(memory_space=pltpu.SMEM)],
        out_specs=vmem,
        scratch_shapes=[
            pltpu.VMEM((2, HEADS, HALF, 2 * HD), BF16),
            pltpu.VMEM((GROUP, SPAN, 2 * HD), BF16),
            pltpu.VMEM((GROUP, HD + 16, SPAN), BF16),
            pltpu.VMEM((2, HEADS, HD + 16, HALF), F32),
            pltpu.VMEM((2, HEADS, 8, HALF), F32),
            pltpu.VMEM((ROWS, HALF), I32),
            pltpu.VMEM((SPAN, HALF), F32),
            pltpu.VMEM((SPAN, HALF), F32),
            pltpu.VMEM((SPAN, HALF), BF16),
            pltpu.VMEM((SPAN, HALF), BF16),
            pltpu.SemaphoreType.DMA((8, 2)),
            pltpu.SemaphoreType.DMA((BACK + 1, 2)),
        ],
        compiler_params=pltpu.CompilerParams(
            collective_id=0, has_side_effects=True, vmem_limit_bytes=48 << 20
        ),
    )(queries, key_rows, value_rows, doc_lengths)


def outgoing(piece_owner, device, pieces, seq_count):
    local_owner = lax.dynamic_slice_in_dim(piece_owner, device * pieces, pieces)
    local_order = jnp.arange(pieces, dtype=jnp.int32)
    earlier = (local_owner[None, :] == local_owner[:, None]) & (
        local_order[None, :] < local_order[:, None]
    )
    slot_rank = jnp.sum(earlier.astype(jnp.int32), axis=1)
    target_slot = jnp.arange(seq_count * 2, dtype=jnp.int32)
    select = local_owner[None, :] * 2 + slot_rank[None, :] == target_slot[:, None]
    return select.astype(jnp.bfloat16)


def incoming(piece_owner, device, pieces):
    piece_total = piece_owner.shape[0]
    piece_ids = jnp.arange(piece_total, dtype=jnp.int32)
    is_mine = piece_owner == device
    mine_rank = jnp.cumsum(is_mine.astype(jnp.int32)) - 1
    my_slots = jnp.arange(pieces, dtype=jnp.int32)
    chosen = is_mine[None, :] & (mine_rank[None, :] == my_slots[:, None])
    held_pieces = jnp.sum(jnp.where(chosen, piece_ids[None, :], 0), axis=1)
    source_dev = held_pieces // pieces
    earlier_mine = (
        is_mine[None, :]
        & (piece_ids[None, :] // pieces == source_dev[:, None])
        & (piece_ids[None, :] < held_pieces[:, None])
    )
    slot_rank = jnp.sum(earlier_mine.astype(jnp.int32), axis=1)
    return source_dev * 2 + slot_rank


def route(row_data, select, arrival_slot):
    pieces = select.shape[1]
    row_width = row_data.shape[1]
    piece_len = row_data.shape[0] // pieces
    stacked = row_data.reshape(pieces, piece_len * row_width)
    rows = jnp.dot(select, stacked, preferred_element_type=F32).astype(row_data.dtype)
    rows = rows.reshape(select.shape[0] * piece_len, row_width)
    arrived = lax.all_to_all(rows, "seq", split_axis=0, concat_axis=0, tiled=True)
    arrived = arrived.reshape(select.shape[0], piece_len, row_width)
    return jnp.take(arrived, arrival_slot, axis=0).reshape(pieces * piece_len, row_width)


def on_device(queries, key_heads, value_heads, out_weight, doc_lengths, piece_owner):
    device = lax.axis_index("seq")
    attended = attention(
        queries.reshape(ROWS, HEADS * HD),
        key_heads.reshape(ROWS, HD),
        value_heads.reshape(ROWS, HD),
        doc_lengths,
    )
    partial_sum = jnp.dot(attended, out_weight, preferred_element_type=F32)
    summed = lax.psum_scatter(
        partial_sum.astype(BF16), "tp", scatter_dimension=1, tiled=True
    )
    select = outgoing(piece_owner, device, 16, 16)
    return route(summed, select, incoming(piece_owner, device, 16))


def solution(mesh):
    placed = (
        P("seq", "tp", None),
        P("seq", "tp", None),
        P("seq", "tp", None),
        P("tp", None),
        P(),
        P(),
    )
    return jax.shard_map(
        on_device, mesh=mesh, in_specs=placed, out_specs=P("seq", "tp"), check_vma=False
    )
```

time: 399 us -> 179 us (0.45)
  waiting for transfers between devices: 184 us -> 82.4 us
  matrix products: 87.9 us -> 11.8 us
  Pallas kernels: 0 us -> 44.4 us
  other arithmetic: 43.3 us -> 2.04 us
  local copies, waits for them, and re-layouts: 43.2 us -> 16.8 us
  starting transfers between devices: 24.9 us -> 7.19 us
    ppermute x30 -> x0, waiting for transfers between devices: 91.5 us -> none  [shifted(): return lax.ppermute(value, axis, pairs)]
    dot_general x34 -> x2, matrix products: 87.9 us -> 11.8 us  [the longest x1 11.3 us: on_device(): partial_sum = jnp.dot(attended, out_weight, preferred_element_type=F32)]
    pallas_call x0 -> x1, Pallas kernels: none -> 44.4 us  [attention(): pl.pallas_call(attend_kernel, out_shape=jax.ShapeDtypeStruct((ROWS, HEADS...]
    reduce_sum x17 -> x0, other arithmetic: 32.6 us -> none  [the longest x16 32.5 us: attend(): run_sum = run_sum * factor + jnp.sum(weights, axis=-1)]
    while x106 -> x0, local copies, waits for them, and re-layouts: 22.5 us -> none
    ppermute x30 -> x0, starting transfers between devices: 15.7 us -> none  [shifted(): return lax.ppermute(value, axis, pairs)]
    all_to_all x1, waiting for transfers between devices: 26 us -> 19.4 us  [route(): lax.all_to_all(rows, 'seq', split_axis=0, concat_axis=0, tiled=True)]
    and x16 -> x0, other arithmetic: 4.37 us -> none  [attend(): (key_pos[None, :] >= query_start[:, None]) & (key_pos[None, :] <= query_p...]
  transfers between devices with their start and end apart: 32 -> 2, of which waited for: 17 -> 2; matrix products, arithmetic and copies ran while one was open for 16% -> 1% of each run, Pallas kernels for 0% -> 0%
where the time goes in v1:
time: 179 us; the launch traced here: 178 us
  waiting for transfers between devices  82.4 us (46%)
  Pallas kernels  44.4 us (25%)
  local copies, waits for them, and re-layouts  16.8 us (9%)
  between operations  13.5 us (8%)
  matrix products  11.8 us (7%)
  starting transfers between devices  7.19 us (4%)
  other arithmetic  2.04 us (1%)
    unnamed x2, waiting for transfers between devices  63 us
    pallas_call x1, Pallas kernels, attention(): pl.pallas_call(attend_kernel, out_shape=jax.ShapeDtypeStruct((ROWS, HEADS...  44.4 us
    all_to_all x1, waiting for transfers between devices, route(): lax.all_to_all(rows, 'seq', split_axis=0, concat_axis=0, tiled=True)  19.4 us
    unnamed x11, local copies, waits for them, and re-layouts  13.9 us
    dot_general x1, matrix products, on_device(): partial_sum = jnp.dot(attended, out_weight, preferred_element_type=F32)  11.3 us
    all_to_all x1, starting transfers between devices, route(): lax.all_to_all(rows, 'seq', split_axis=0, concat_axis=0, tiled=True)  7.18 us
  transfers between devices with their start and end apart: 2, of which 2 were waited for; matrix products, arithmetic and copies ran while one was open for 1% of the time, Pallas kernels for 0%

profile of v1, /device:TPU:1, one launch (start us, length us, event | category | flops | bytes accessed | tf_op | source)
XLA Modules:
  0.0 178.2 jit_solution(4990842611461192815)
XLA Ops:
  6.5 0.0 reduce-scatter.4.cloned.1.call-start
  6.5 1.5 copy.11
  8.0 0.0 copy-start
  8.0 0.9 copy-done
  8.9 0.0 copy-start.1
  8.9 0.9 copy-done.1
  9.8 0.0 copy-start.2
  9.9 0.7 copy-done.2
  10.5 44.4 %shard_map.64 = bf16[512,1024]{1,0:T(8,128)(2,1)S(1)} custom-call(bf16[512,1024]{1,0:T(8,128)(2,1)S(1)} %bitcast.34, bf16[512,128]{1,0:T(8,128)(2,1)S(1)} %bitcast.35, bf16[512,128]{1,0:T(8,128)(2,1)S(1)} %bitcast.36, s32[4]{0:T(128)S(1)} %copy-done.2), custom_call_target="tpu_custom_call" | custom-call | tf_op jit(solution)/shard_map/pallas_call | solution.py:247
  54.9 11.3 %convolution_convert_fusion.1 = bf16[512,5120]{1,0:T(8,128)(2,1)} fusion(bf16[512,1024]{1,0:T(8,128)(2,1)S(1)} %shard_map.64, bf16[1024,5120]{1,0:T(8,128)(2,1)} %param.9), kind=kOutput, calls=%fused_computation.2 | convolution fusion | flops 5371330560 | bytes 16777216 | tf_op jit(solution)/shard_map/dot_general | solution.py:322
  66.3 7.9 %copy.7 = bf16[512,5120]{0,1:T(8,128)(2,1)} copy(bf16[512,5120]{1,0:T(8,128)(2,1)} %convolution_convert_fusion.1) | data formatting | bytes 10485760
  74.2 0.0 copy-start.3
  74.2 0.0 reduce-scatter.4.cloned.1.call-update
  74.2 0.6 copy-done.3
  74.9 0.1 dynamic_slice.3
  75.0 0.3 reduce-window.9
  75.3 0.1 slice.7
  75.4 0.1 slice_reduce_fusion
  75.5 0.2 convert_reduce_fusion.1
  75.7 0.1 multiply_add_fusion
  75.8 63.0 %reduce-scatter.4.cloned.1.call-done = bf16[640,512]{1,0:T(8,128)(2,1)} async-done(((bf16[5120,512]{1,0:T(8,128)(2,1)}), bf16[640,512]{1,0:T(8,128)(2,1)}) %reduce-scatter.4.cloned.1.call-update) | async-done | bytes 655376
  138.8 1.4 copy.8
  140.2 0.3 reshape.175
  140.5 0.5 convolution_convert_fusion
  141.0 1.5 all_to_all.6
  142.4 7.2 %all-to-all-start = ((bf16[16,64,640]{2,1,0:T(8,128)(2,1)}), bf16[16,64,640]{2,1,0:T(8,128)(2,1)S(1)}, u32[]{:S(2)}, u32[]{:S(2)}) async-start(bf16[16,64,640]{2,1,0:T(8,128)(2,1)} %all_to_all.6), calls=%async_computation | async-start | bytes 2621440 | tf_op jit(solution)/shard_map/all_to_all | solution.py:309
  149.6 0.1 add_bitcast_fusion
  149.7 0.1 select_reduce_fusion
  149.8 0.2 convert_reduce_fusion
  150.0 0.1 broadcast_in_dim.47
  150.1 0.1 broadcast_in_dim.48
  150.2 19.4 %all-to-all-done = bf16[16,64,640]{2,1,0:T(8,128)(2,1)S(1)} async-done(((bf16[16,64,640]{2,1,0:T(8,128)(2,1)}), bf16[16,64,640]{2,1,0:T(8,128)(2,1)S(1)}, u32[]{:S(2)}, u32[]{:S(2)}) %all-to-all-start) | async-done | bytes 1310752 | tf_op jit(solution)/shard_map/all_to_all | solution.py:309
  169.6 0.7 gather_fusion
  170.3 1.0 bitcast_select_fusion
  (7 shorter events, 0.1 us)
Async XLA Ops:
  6.5 132.2 %reduce-scatter.4.cloned.1.call-start = ((), (), s32[]{:S(2)}) async-start(), calls=%async_computation.2 | async-start | bytes 5898240
  8.0 0.9 copy-start
  8.9 0.9 copy-start.1
  9.8 0.7 copy-start.2
  74.2 0.7 copy-start.3
  142.4 27.2 %all-to-all-start = ((bf16[16,64,640]{2,1,0:T(8,128)(2,1)}), bf16[16,64,640]{2,1,0:T(8,128)(2,1)S(1)}, u32[]{:S(2)}, u32[]{:S(2)}) async-start(bf16[16,64,640]{2,1,0:T(8,128)(2,1)} %all_to_all.6), calls=%async_computation | async-start | bytes 2621440 | tf_op jit(solution)/shard_map/all_to_all | solution.py:309
Sparse Core Ops, SparseCore 0:
  74.4 64.3 reduce-scatter.3

commit v2 on v1

--- a/solution.py
+++ b/solution.py
@@ -12,10 +12,18 @@
 ROWS = 512
 HEADS = 8
 HD = 128
-HALF = 256
+WIDTH = 640
+CHUNK = 128
+CHUNKS = ROWS // CHUNK
+PAIRS = HEADS // 2
 GROUP = 3
 SPAN = GROUP * ROWS
 BACK = 8
+TILES = CHUNKS * GROUP * PAIRS
+FINISH = {7: 0, 13: 1, 19: 2, 25: 3}
+PASS_ON = {10: 1, 13: 2, 17: 3, 20: 5, 23: 9, 25: 6, 26: 10, 27: 13, 28: 7, 29: 11, 30: 14, 31: 15}
+LAST = {20: 0, 30: 1, 31: 2, 32: 3}
+STEPS = 33
 SCORE = HD**-0.5 * 1.4426950408889634
 MESH = pl.DeviceIdType.MESH
 
@@ -46,10 +54,21 @@
     return doc
 
 
+def pick(index, table):
+    found = -1
+    for key, value in table.items():
+        found = jnp.where(index == key, value, found)
+    return found
+
+
 def attend_kernel(
-    q_ref, k_ref, v_ref, len_ref, o_ref, qx, kx, vx, acc, top, diff, s0, s1, p0, p1, send, recv
+    q_ref, k_ref, v_ref, len_ref, w_hbm, o_ref,
+    qx, kx, vx, acc, top, fac, diff, s0, s1, p0, p1, att, w, out_buf, ring, got_z,
+    send, recv, w_sem, ring_send, ring_recv, z_send, z_recv,
 ):
     s, z, core, at = places()
+    t = lax.axis_index("tp")
+    z_lo, y = t // 4, t % 4
     sibling, next_x, prev_x, far_x, other_z = (
         at(0, 0, 1),
         at(1, 0, 0),
@@ -57,15 +76,18 @@
         at(2, 0, 0),
         at(0, 1, 0),
     )
+    ahead, behind, partner = z_lo * 4 + (y + 1) % 4, z_lo * 4 + (y + 3) % 4, (1 - z_lo) * 4 + y
+    load_w = pltpu.make_async_copy(w_hbm, w, w_sem)
+    load_w.start()
     barrier = pltpu.get_barrier_semaphore()
     for peer in (sibling, next_x, prev_x, far_x, other_z):
         pl.semaphore_signal(barrier, inc=1, device_id={"seq": peer}, device_id_type=MESH)
+    for peer in (ahead, behind, partner):
+        pl.semaphore_signal(barrier, inc=1, device_id={"tp": peer}, device_id_type=MESH)
 
     kx[0, :ROWS, :HD] = k_ref[...]
     vx[0, :HD, :ROWS] = v_ref[...].T
-    pl.semaphore_wait(barrier, 5)
-
-    sends = []
+    pl.semaphore_wait(barrier, 8)
 
     def copies(index, source, target, peer):
         for part, (a, b) in enumerate(zip(slot(kx, vx, source), slot(kx, vx, target))):
@@ -113,10 +135,11 @@
     row = lax.broadcasted_iota(I32, (ROWS, HD), 0)
     mine = jnp.where(doc_of(ends, row + s * ROWS) == lane, MASKED, 0.0).astype(BF16)
     for h in range(HEADS):
-        for half in range(2):
-            rows = pl.ds(half * HALF, HALF)
-            qx[half, h, :, :HD] = q_ref[rows, pl.ds(h * HD, HD)]
-            qx[half, h, :, HD:] = mine[half * HALF : (half + 1) * HALF]
+        for c in range(CHUNKS):
+            rows = pl.ds(c * CHUNK, CHUNK)
+            place = pl.ds(h % 2 * CHUNK, CHUNK)
+            qx[c, h // 2, place, :HD] = q_ref[rows, pl.ds(h * HD, HD)]
+            qx[c, h // 2, place, HD:] = mine[c * CHUNK : (c + 1) * CHUNK]
 
     def mark(delta, _):
         start = pl.multiple_of((delta % GROUP) * ROWS, ROWS)
@@ -127,11 +150,13 @@
     lax.fori_loop(0, BACK + 1, mark, 0)
     for g in range(GROUP):
         vx[g, HD:, :] = jnp.ones((16, SPAN), BF16)
-    diff[...] = lax.broadcasted_iota(I32, (ROWS, HALF), 0) - lax.broadcasted_iota(
-        I32, (ROWS, HALF), 1
+    diff[...] = lax.broadcasted_iota(I32, (ROWS, 2 * CHUNK), 0) - (
+        lax.broadcasted_iota(I32, (ROWS, 2 * CHUNK), 1) % CHUNK
     )
     acc[...] = jnp.zeros_like(acc)
+    fac[...] = jnp.zeros_like(fac)
     top[...] = jnp.full_like(top, MASKED)
+    p1[...] = jnp.zeros_like(p1)
 
     arrived(4)
 
@@ -165,11 +190,91 @@
 
     scores, weights = (s0, s1), (p0, p1)
 
-    def matrix(a, b):
-        return lax.dot_general(a, b, (((1,), (1,)), ((), ())), preferred_element_type=F32)
-
-    def one_pass(step, _):
-        @pl.when(step == 1)
+    def tile(n):
+        return n // (GROUP * PAIRS), n // PAIRS % GROUP, n % PAIRS
+
+    def score(n, out):
+        c, g, p = tile(n)
+        limit = c * CHUNK + g * SPAN
+        qh = qx[c, p]
+        both = (((1,), (1,)), ((), ()))
+        near = lax.dot_general(kx[g, :ROWS, :], qh, both, preferred_element_type=F32)
+        out[:ROWS] = jnp.where(diff[...] <= limit, near, MASKED)
+        out[ROWS:] = lax.dot_general(kx[g, ROWS:, :], qh, both, preferred_element_type=F32)
+
+    def weigh(n, par):
+        c, g, p = tile(n)
+        sc = scores[par][...]
+        before = jnp.where(g == 0, MASKED, top[p, :1, :])
+        now = jnp.maximum(before, jnp.max(sc, axis=0, keepdims=True))
+        weights[par][...] = jnp.exp2((sc - now) * SCORE).astype(BF16)
+        fac[par, :1, :] = jnp.where(g == 0, 0.0, jnp.exp2((before - now) * SCORE))
+        top[p, :1, :] = now
+
+    def mix(n, par):
+        c, g, p = tile(n)
+        acc[c % 2, p] = acc[c % 2, p] * fac[par, :1, :] + jnp.dot(
+            vx[g], weights[par][...], preferred_element_type=F32
+        )
+
+    def ring_copy(c, k, way):
+        return pltpu.make_async_remote_copy(
+            src_ref=ring.at[c, k, way],
+            dst_ref=ring.at[c, k + 1, way],
+            send_sem=ring_send.at[c, k, way],
+            recv_sem=ring_recv.at[c, k, way],
+            device_id={"tp": (ahead, behind)[way]},
+            device_id_type=MESH,
+        )
+
+    def z_copy(c):
+        return pltpu.make_async_remote_copy(
+            src_ref=ring.at[c, 3, 1 - z_lo],
+            dst_ref=got_z.at[c],
+            send_sem=z_send.at[c],
+            recv_sem=z_recv.at[c],
+            device_id={"tp": partner},
+            device_id_type=MESH,
+        )
+
+    def share(c, k, way):
+        owner = (y + 3 - k) % 4 if way == 0 else (y + 1 + k) % 4
+        column = pl.multiple_of((way * 4 + owner) * WIDTH, HD)
+        return jnp.dot(att[c], w[:, pl.ds(column, WIDTH)], preferred_element_type=F32)
+
+    def finish(c):
+        for h in range(HEADS):
+            cols = pl.ds(h % 2 * CHUNK, CHUNK)
+            part = acc[c % 2, h // 2, :, cols]
+            value = part[:HD] / part[HD : HD + 1]
+            att[c, :, pl.ds(h * HD, HD)] = value.T.astype(BF16)
+        for way in range(2):
+            ring[c, 0, way] = share(c, 0, way).astype(BF16)
+            ring_copy(c, 0, way).start()
+
+    def pass_on(c, k):
+        for way in range(2):
+            mine = share(c, k, way)
+            ring_copy(c, k - 1, way).wait_recv()
+            ring[c, k, way] = (ring[c, k, way].astype(F32) + mine).astype(BF16)
+
+            @pl.when(k < 3)
+            def _():
+                ring_copy(c, k, way).start()
+
+        @pl.when(k == 3)
+        def _():
+            z_copy(c).start()
+
+    def last(c):
+        z_copy(c).wait_recv()
+        total = ring[c, 3, z_lo].astype(F32) + got_z[c].astype(F32)
+        out_buf[pl.ds(pl.multiple_of(c * CHUNK, CHUNK), CHUNK), :] = total.astype(BF16)
+
+    score(0, s0)
+
+    def step(i, _):
+        @pl.when(i == 1)
         def _():
             arrived(8)
 
@@ -181,7 +286,10 @@
             def _():
                 to_sibling(3)
 
-        @pl.when(step == 2)
+            arrived(3)
+            arrived(5)
+
+        @pl.when(i == 3)
         def _():
             arrived(6)
 
@@ -193,46 +301,47 @@
             def _():
                 to_sibling(2)
 
-            arrived(3)
-            arrived(5)
-
-        @pl.when(step == 3)
-        def _():
             arrived(7)
 
-        g = jnp.where(step < 2, 0, 1 + step % 2)
-        half = jnp.where(step < 2, step, (step - 2) // 2)
-        limit = half * HALF + g * SPAN
-        factor = {}
-        for i in range(HEADS + 2):
-            if i < HEADS:
-                out = scores[i % 2]
-                qh = qx[half, i]
-                out[:ROWS] = jnp.where(
-                    diff[...] <= limit, matrix(kx[g, :ROWS, :], qh), MASKED
-                )
-                out[ROWS:] = matrix(kx[g, ROWS:, :], qh)
-            if 0 <= i - 1 < HEADS:
-                h = i - 1
-                sc = scores[h % 2][...]
-                before = top[half, h, :1, :]
-                now = jnp.maximum(before, jnp.max(sc, axis=0, keepdims=True))
-                weights[h % 2][...] = jnp.exp2((sc - now) * SCORE).astype(BF16)
-                factor[h] = jnp.exp2((before - now) * SCORE)
-                top[half, h, :1, :] = now
-            if 0 <= i - 2 < HEADS:
-                h = i - 2
-                acc[half, h] = acc[half, h] * factor[h] + jnp.dot(
-                    vx[g], weights[h % 2][...], preferred_element_type=F32
-                )
+        @pl.when(i == 7)
+        def _():
+            load_w.wait()
+
+        ready = pick(i, FINISH)
+
+        @pl.when(ready >= 0)
+        def _():
+            finish(ready)
+
+        move = pick(i, PASS_ON)
+
+        @pl.when(move >= 0)
+        def _():
+            pass_on(move // 4, move % 4)
+
+        done = pick(i, LAST)
+
+        @pl.when(done >= 0)
+        def _():
+            last(done)
+
+        @pl.when(i < TILES // 2)
+        def _():
+            score(2 * i + 1, s1)
+            weigh(2 * i, 0)
+            mix(jnp.maximum(2 * i - 1, 0) + jnp.where(i == 0, PAIRS - 1, 0), 1)
+            score(jnp.minimum(2 * i + 2, TILES - 1), s0)
+            weigh(2 * i + 1, 1)
+            mix(2 * i, 0)
+
+        @pl.when(i == TILES // 2)
+        def _():
+            mix(TILES - 1, 1)
+
         return 0
 
-    lax.fori_loop(0, 6, one_pass, 0)
-
-    for half in range(2):
-        for h in range(HEADS):
-            value = acc[half, h, :HD, :] / acc[half, h, HD : HD + 1, :]
-            o_ref[pl.ds(half * HALF, HALF), pl.ds(h * HD, HD)] = value.T.astype(BF16)
+    lax.fori_loop(0, STEPS, step, 0)
+    o_ref[...] = out_buf[...]
 
     for index in range(4):
         for copy in copies(index, 0, 1, sibling):
@@ -240,33 +349,55 @@
     for i in range(4):
         for copy in copies(4 + i, 0, 1, sibling):
             copy.wait_send()
-
-
-def attention(queries, key_rows, value_rows, doc_lengths):
+    for c in range(CHUNKS):
+        for k in range(3):
+            for way in range(2):
+                ring_copy(c, k, way).wait_send()
+        z_copy(c).wait_send()
+
+
+def attention(queries, key_rows, value_rows, doc_lengths, out_weight):
     vmem = pl.BlockSpec(memory_space=pltpu.VMEM)
     return pl.pallas_call(
         attend_kernel,
-        out_shape=jax.ShapeDtypeStruct((ROWS, HEADS * HD), BF16),
-        in_specs=[vmem, vmem, vmem, pl.BlockSpec(memory_space=pltpu.SMEM)],
+        out_shape=jax.ShapeDtypeStruct((ROWS, WIDTH), BF16),
+        in_specs=[
+            vmem,
+            vmem,
+            vmem,
+            pl.BlockSpec(memory_space=pltpu.SMEM),
+            pl.BlockSpec(memory_space=pl.ANY),
+        ],
         out_specs=vmem,
         scratch_shapes=[
-            pltpu.VMEM((2, HEADS, HALF, 2 * HD), BF16),
+            pltpu.VMEM((CHUNKS, PAIRS, 2 * CHUNK, 2 * HD), BF16),
             pltpu.VMEM((GROUP, SPAN, 2 * HD), BF16),
             pltpu.VMEM((GROUP, HD + 16, SPAN), BF16),
-            pltpu.VMEM((2, HEADS, HD + 16, HALF), F32),
-            pltpu.VMEM((2, HEADS, 8, HALF), F32),
-            pltpu.VMEM((ROWS, HALF), I32),
-            pltpu.VMEM((SPAN, HALF), F32),
-            pltpu.VMEM((SPAN, HALF), F32),
-            pltpu.VMEM((SPAN, HALF), BF16),
-            pltpu.VMEM((SPAN, HALF), BF16),
+            pltpu.VMEM((2, PAIRS, HD + 16, 2 * CHUNK), F32),
+            pltpu.VMEM((PAIRS, 8, 2 * CHUNK), F32),
+            pltpu.VMEM((2, 8, 2 * CHUNK), F32),
+            pltpu.VMEM((ROWS, 2 * CHUNK), I32),
+            pltpu.VMEM((SPAN, 2 * CHUNK), F32),
+            pltpu.VMEM((SPAN, 2 * CHUNK), F32),
+            pltpu.VMEM((SPAN, 2 * CHUNK), BF16),
+            pltpu.VMEM((SPAN, 2 * CHUNK), BF16),
+            pltpu.VMEM((CHUNKS, CHUNK, HEADS * HD), BF16),
+            pltpu.VMEM((HEADS * HD, 8 * WIDTH), BF16),
+            pltpu.VMEM((ROWS, WIDTH), BF16),
+            pltpu.VMEM((CHUNKS, 4, 2, CHUNK, WIDTH), BF16),
+            pltpu.VMEM((CHUNKS, CHUNK, WIDTH), BF16),
             pltpu.SemaphoreType.DMA((8, 2)),
             pltpu.SemaphoreType.DMA((BACK + 1, 2)),
+            pltpu.SemaphoreType.DMA,
+            pltpu.SemaphoreType.DMA((CHUNKS, 3, 2)),
+            pltpu.SemaphoreType.DMA((CHUNKS, 3, 2)),
+            pltpu.SemaphoreType.DMA((CHUNKS,)),
+            pltpu.SemaphoreType.DMA((CHUNKS,)),
         ],
         compiler_params=pltpu.CompilerParams(
-            collective_id=0, has_side_effects=True, vmem_limit_bytes=48 << 20
+            collective_id=0, has_side_effects=True, vmem_limit_bytes=56 << 20
         ),
-    )(queries, key_rows, value_rows, doc_lengths)
+    )(queries, key_rows, value_rows, doc_lengths, out_weight)
 
 
 def outgoing(piece_owner, device, pieces, seq_count):
@@ -313,15 +444,12 @@
 
 def on_device(queries, key_heads, value_heads, out_weight, doc_lengths, piece_owner):
     device = lax.axis_index("seq")
-    attended = attention(
+    summed = attention(
         queries.reshape(ROWS, HEADS * HD),
         key_heads.reshape(ROWS, HD),
         value_heads.reshape(ROWS, HD),
         doc_lengths,
-    )
-    partial_sum = jnp.dot(attended, out_weight, preferred_element_type=F32)
-    summed = lax.psum_scatter(
-        partial_sum.astype(BF16), "tp", scatter_dimension=1, tiled=True
+        out_weight,
     )
     select = outgoing(piece_owner, device, 16, 16)
     return route(summed, select, incoming(piece_owner, device, 16))

time: 179 us -> 133 us (0.74)
  waiting for transfers between devices: 82.4 us -> 18.8 us
  Pallas kernels: 44.4 us -> 97.5 us
  between operations: 13.5 us -> 0.09 us
  matrix products: 11.8 us -> 0.48 us
  local copies, waits for them, and re-layouts: 16.8 us -> 6.47 us
    unnamed x2 -> x0, waiting for transfers between devices: 63 us -> none
    pallas_call x1, Pallas kernels: 44.4 us -> 97.5 us  [attention(): pl.pallas_call(attend_kernel, out_shape=jax.ShapeDtypeStruct((ROWS, WIDTH...]
    unnamed x11 -> x3, local copies, waits for them, and re-layouts: 13.9 us -> 2.5 us
    dot_general x1 -> x0, matrix products: 11.3 us -> none  [on_device(): partial_sum = jnp.dot(attended, out_weight, preferred_element_type=F32)]
  transfers between devices with their start and end apart: 2 -> 1, of which waited for: 2 -> 1; matrix products, arithmetic and copies ran while one was open for 1% -> 1% of each run, Pallas kernels for 0% -> 0%
where the time goes in v2:
time: 133 us; the launch traced here: 132 us
  Pallas kernels  97.5 us (73%)
  waiting for transfers between devices  18.8 us (14%)
  starting transfers between devices  6.88 us (5%)
  local copies, waits for them, and re-layouts  6.47 us (5%)
  other arithmetic  2.05 us (2%)
    pallas_call x1, Pallas kernels, attention(): pl.pallas_call(attend_kernel, out_shape=jax.ShapeDtypeStruct((ROWS, WIDTH...  97.5 us
    all_to_all x1, waiting for transfers between devices, route(): lax.all_to_all(rows, 'seq', split_axis=0, concat_axis=0, tiled=True)  18.8 us
    all_to_all x1, starting transfers between devices, route(): lax.all_to_all(rows, 'seq', split_axis=0, concat_axis=0, tiled=True)  6.88 us
  transfers between devices with their start and end apart: 1, of which 1 were waited for; matrix products, arithmetic and copies ran while one was open for 1% of the time, Pallas kernels for 0%

profile of v2, /device:TPU:1, one launch (start us, length us, event | category | flops | bytes accessed | tf_op | source)
XLA Modules:
  0.0 132.3 jit_solution(9734560922005655302)
XLA Ops:
  0.0 2.5 %copy.9 = bf16[64,8,8,128]{3,1,2,0:T(8,128)(2,1)} copy(bf16[64,8,8,128]{3,2,1,0:T(8,128)(2,1)} %bitcast.32) | data formatting | bytes 2097152
  2.5 97.5 %shard_map.64 = bf16[512,640]{1,0:T(8,128)(2,1)} custom-call(bf16[512,1024]{1,0:T(8,128)(2,1)} %bitcast.30, bf16[512,128]{1,0:T(8,128)(2,1)} %bitcast.33, bf16[512,128]{1,0:T(8,128)(2,1)} %bitcast.34, s32[4]{0:T(128)} %len_ref.1, bf16[1024,5120]{1,0:T(8,128)(2,1)} %w_hbm.1), custom_call_target="tpu_custom_call" | custom-call | tf_op jit(solution)/shard_map/pallas_call | solution.py:361
  100.0 0.0 copy-start
  100.0 1.4 %reshape.175 = bf16[16,20480]{1,0:T(8,128)(2,1)S(1)} reshape(bf16[512,640]{1,0:T(8,128)(2,1)} %shard_map.64) | data formatting | bytes 1310720 | tf_op jit(solution)/shard_map/reshape | solution.py:437
  101.4 0.0 copy-done
  101.4 0.1 dynamic_slice.3
  101.5 0.2 convert_reduce_fusion.1
  101.7 0.1 multiply_add_fusion
  101.8 0.5 convolution_convert_fusion
  102.3 1.5 %all_to_all.6 = bf16[16,64,640]{2,1,0:T(8,128)(2,1)} reshape(bf16[32,20480]{1,0:T(8,128)(2,1)S(1)} %convolution_convert_fusion) | data formatting | bytes 2621440 | tf_op jit(solution)/shard_map/all_to_all | solution.py:440
  103.8 6.9 %all-to-all-start = ((bf16[16,64,640]{2,1,0:T(8,128)(2,1)}), bf16[16,64,640]{2,1,0:T(8,128)(2,1)S(1)}, u32[]{:S(2)}, u32[]{:S(2)}) async-start(bf16[16,64,640]{2,1,0:T(8,128)(2,1)} %all_to_all.6), calls=%async_computation | async-start | bytes 2621440 | tf_op jit(solution)/shard_map/all_to_all | solution.py:440
  110.6 0.3 reduce-window.9
  111.0 0.1 slice.7
  111.1 0.1 slice_reduce_fusion
  111.2 0.1 add_bitcast_fusion
  111.3 0.1 select_reduce_fusion
  111.4 0.2 convert_reduce_fusion
  111.6 0.1 broadcast_in_dim.47
  111.7 0.1 broadcast_in_dim.48
  111.8 18.8 %all-to-all-done = bf16[16,64,640]{2,1,0:T(8,128)(2,1)S(1)} async-done(((bf16[16,64,640]{2,1,0:T(8,128)(2,1)}), bf16[16,64,640]{2,1,0:T(8,128)(2,1)S(1)}, u32[]{:S(2)}, u32[]{:S(2)}) %all-to-all-start) | async-done | bytes 1310752 | tf_op jit(solution)/shard_map/all_to_all | solution.py:440
  130.6 0.7 gather_fusion
  131.3 1.0 bitcast_select_fusion
  (7 shorter events, 0.1 us)
Async XLA Ops:
  100.0 1.4 %copy-start = (s32[256]{0:T(256)S(1)}, s32[256]{0:T(256)}, u32[]{:S(2)}) copy-start(s32[256]{0:T(256)} %param.11) | copy-start | bytes 3076
  103.8 26.9 %all-to-all-start = ((bf16[16,64,640]{2,1,0:T(8,128)(2,1)}), bf16[16,64,640]{2,1,0:T(8,128)(2,1)S(1)}, u32[]{:S(2)}, u32[]{:S(2)}) async-start(bf16[16,64,640]{2,1,0:T(8,128)(2,1)} %all_to_all.6), calls=%async_computation | async-start | bytes 2621440 | tf_op jit(solution)/shard_map/all_to_all | solution.py:440

commit v3 on v2

v3 whole, which is shorter than its diff:
```python
import functools

import jax
import jax.numpy as jnp
from jax import lax
from jax.experimental import pallas as pl
from jax.experimental.pallas import tpu as pltpu
from jax.sharding import PartitionSpec as P

MASKED = -1e30
BF16, F32, I32 = jnp.bfloat16, jnp.float32, jnp.int32
ROWS = 512
HEADS = 8
HD = 128
WIDTH = 640
CHUNK = 128
CHUNKS = ROWS // CHUNK
PAIRS = HEADS // 2
GROUP = 4
SPAN = GROUP * ROWS
BACK = 8
PIECE = 32
SEQ = 16
TILES = 2 * CHUNKS * PAIRS
FINISH = {7: 0, 9: 1, 13: 2, 17: 3}
PASS_ON = {9: 1, 11: 2, 13: 5, 15: 3, 16: 6, 18: 9, 19: 7, 20: 13, 21: 10, 22: 14, 23: 11, 24: 15}
LAST = {17: 0, 21: 1, 24: 2, 25: 3}
STEPS = 26
SCORE = HD**-0.5 * 1.4426950408889634
MESH = pl.DeviceIdType.MESH


def places():
    s = lax.axis_index("seq")
    x, z, core = s // 4, (s // 2) % 2, s % 2

    def at(step, flip_z, flip_core):
        return ((x + step) % 4) * 4 + ((z + flip_z) % 2) * 2 + (core + flip_core) % 2

    return s, z, core, at


def slot(ref_k, ref_v, delta):
    g, r = (delta - 1) // GROUP, (delta - 1) % GROUP
    start = pl.multiple_of(r * ROWS, ROWS)
    return (
        ref_k.at[g, pl.ds(start, ROWS), pl.ds(0, HD)],
        ref_v.at[g, pl.ds(0, HD), pl.ds(start, ROWS)],
    )


def doc_of(ends, positions):
    doc = jnp.where(positions < 0, -1, 0)
    for end in ends:
        doc = doc + jnp.where(positions >= end, 1, 0)
    return doc


def pick(index, table):
    found = -1
    for key, value in table.items():
        found = jnp.where(index == key, value, found)
    return found


def attend_kernel(
    q_ref, k_ref, v_ref, len_ref, owner_ref, w_hbm, o_ref,
    qx, k_own, v_own, kx, vx, acc, top, fac, diff, s0, s1, p0, p1, att, w, ring, got_z,
    rows, parcels, parcels_in, out_from, in_from,
    send, recv, w_sem, ring_send, ring_recv, z_send, z_recv, parcel_send, parcel_recv,
):
    s, z, core, at = places()
    t = lax.axis_index("tp")
    z_lo, y = t // 4, t % 4
    sibling, next_x, prev_x, far_x, other_z = (
        at(0, 0, 1),
        at(1, 0, 0),
        at(3, 0, 0),
        at(2, 0, 0),
        at(0, 1, 0),
    )
    ahead, behind, partner = z_lo * 4 + (y + 1) % 4, z_lo * 4 + (y + 3) % 4, (1 - z_lo) * 4 + y
    load_w = pltpu.make_async_copy(w_hbm, w, w_sem)
    load_w.start()
    barrier = pltpu.get_barrier_semaphore()
    for k in range(1, SEQ):
        pl.semaphore_signal(
            barrier, inc=1, device_id={"seq": (s + k) % SEQ}, device_id_type=MESH
        )
    for peer in (ahead, behind, partner):
        pl.semaphore_signal(barrier, inc=1, device_id={"tp": peer}, device_id_type=MESH)

    k_own[:, :HD] = k_ref[...]
    v_own[:HD] = v_ref[...].T
    pl.semaphore_wait(barrier, SEQ - 1 + 3)

    def copy_of(index, source, target, peer, part):
        if source is None:
            a = (k_own.at[:, pl.ds(0, HD)], v_own.at[pl.ds(0, HD), :])[part]
        else:
            a = slot(kx, vx, source)[part]
        return pltpu.make_async_remote_copy(
            src_ref=a,
            dst_ref=slot(kx, vx, target)[part],
            send_sem=send.at[index, part],
            recv_sem=recv.at[target, part],
            device_id={"seq": peer},
            device_id_type=MESH,
        )

    def copies(index, source, target, peer):
        return [copy_of(index, source, target, peer, part) for part in range(2)]

    def go(index, source, target, peer, part):
        copy_of(index, source, target, peer, part).start()

    def arrived(target, part):
        copy_of(0, None, target, sibling, part).wait_recv()

    def pass_block(name, part):
        if name == 4:
            @pl.when(z == 1)
            def _():
                go(2, 4, 2, other_z, part)

            @pl.when(z == 0)
            def _():
                go(3, 4, 6, other_z, part)

        if name == 8:
            @pl.when(z == 1)
            def _():
                go(3, 8, 6, other_z, part)

        if name < 8:
            @pl.when(core == 0)
            def _():
                go(4 + name // 2, name, name + 1, sibling, part)

        @pl.when(core == 1)
        def _():
            go(3 + name // 2, name, name - 1, sibling, part)

    for part in range(2):
        go(0, None, 4, next_x, part)

        @pl.when(z == 0)
        def _():
            go(2, None, 2, other_z, part)

        @pl.when(core == 0)
        def _():
            go(4, None, 1, sibling, part)

    ends = []
    total = 0
    for d in range(4):
        total = total + len_ref[d]
        ends.append(total)
    lane = lax.broadcasted_iota(I32, (ROWS, HD), 1)
    row = lax.broadcasted_iota(I32, (ROWS, HD), 0)
    mine = jnp.where(doc_of(ends, row + s * ROWS) == lane, MASKED, 0.0).astype(BF16)
    for h in range(HEADS):
        for c in range(CHUNKS):
            queries = pl.ds(c * CHUNK, CHUNK)
            side = pl.ds(h % 2 * CHUNK, CHUNK)
            qx[c, h // 2, side, :HD] = q_ref[queries, pl.ds(h * HD, HD)]
            qx[c, h // 2, side, HD:] = mine[c * CHUNK : (c + 1) * CHUNK]

    own_seen = doc_of(ends, row + s * ROWS) == lane
    k_own[:, HD:] = jnp.where(own_seen, 0.0, 1.0).astype(BF16)
    v_own[HD:] = jnp.ones((16, ROWS), BF16)

    def mark(delta, _):
        start = pl.multiple_of((delta - 1) % GROUP * ROWS, ROWS)
        seen = doc_of(ends, row + (s - delta) * ROWS) == lane
        kx[(delta - 1) // GROUP, pl.ds(start, ROWS), HD:] = jnp.where(seen, 0.0, 1.0).astype(BF16)
        return 0

    lax.fori_loop(1, BACK + 1, mark, 0)
    for g in range(2):
        vx[g, HD:, :] = jnp.ones((16, SPAN), BF16)
    diff[...] = lax.broadcasted_iota(I32, (ROWS, 2 * CHUNK), 0) - (
        lax.broadcasted_iota(I32, (ROWS, 2 * CHUNK), 1) % CHUNK
    )
    fac[...] = jnp.ones_like(fac)
    p1[...] = jnp.zeros_like(p1)

    scores, weights = (s0, s1), (p0, p1)

    both = (((1,), (1,)), ((), ()))

    def own_pass(i, _):
        @pl.when(i == 3)
        def _():
            arrived(4, 0)
            pass_block(4, 0)

        @pl.when(i == 5)
        def _():
            arrived(4, 1)
            pass_block(4, 1)

        c = i // 2
        pairs = (i % 2 * 2, i % 2 * 2 + 1)
        for par, p in enumerate(pairs):
            near = lax.dot_general(k_own[...], qx[c, p], both, preferred_element_type=F32)
            scores[par][:ROWS] = jnp.where(diff[...] <= c * CHUNK, near, MASKED)
        for par, p in enumerate(pairs):
            sc = scores[par][:ROWS]
            now = jnp.max(sc, axis=0, keepdims=True)
            top[c, p, :1, :] = now
            weight = jnp.exp2((sc - now) * SCORE).astype(BF16)
            acc[c, p] = jnp.dot(v_own[...], weight, preferred_element_type=F32)
        return 0

    lax.fori_loop(0, 2 * CHUNKS, own_pass, 0)

    for part in range(2):
        copy_of(0, None, 4, next_x, part).wait_send()
        go(1, None, 8, far_x, part)

    own = [owner_ref[s * 16 + k] for k in range(16)]
    place = []
    for k in range(16):
        rank = 0
        for j in range(k):
            rank = rank + jnp.where(own[j] == own[k], 1, 0)
        place.append(2 * own[k] + rank)
    for n in range(2 * SEQ):
        piece = 0
        for k in range(16):
            piece = piece + jnp.where(place[k] == n, k, 0)
        out_from[n] = piece
    before = 0
    found = [0] * 16
    for source in range(SEQ):
        count = 0
        for k in range(16):
            count = count + jnp.where(owner_ref[source * 16 + k] == s, 1, 0)
        far = (s - source + SEQ) % SEQ
        for j in range(16):
            for r in range(2):
                hit = (before + r == j) & (r < count)
                found[j] = found[j] + jnp.where(hit, 2 * far + r, 0)
        before = before + count
    for j in range(16):
        in_from[j] = found[j]

    for part in range(2):
        arrived(2, part)
        pass_block(2, part)
    for part in range(2):
        arrived(1, part)
        arrived(3, part)

    def tile(n):
        b = n // PAIRS
        c = jnp.where(b < 4, b % 2, b // 2)
        g = jnp.where(b < 4, b // 2, b % 2)
        return c, g, n % PAIRS

    def score(n, out):
        c, g, p = tile(n)
        out[...] = lax.dot_general(kx[g], qx[c, p], both, preferred_element_type=F32)

    def weigh(n, par):
        c, g, p = tile(n)
        sc = scores[par][...]
        before = top[c, p, :1, :]
        now = jnp.maximum(before, jnp.max(sc, axis=0, keepdims=True))
        weights[par][...] = jnp.exp2((sc - now) * SCORE).astype(BF16)
        fac[par, :1, :] = jnp.exp2((before - now) * SCORE)
        top[c, p, :1, :] = now

    def mix(n, par):
        c, g, p = tile(n)
        acc[c, p] = acc[c, p] * fac[par, :1, :] + jnp.dot(
            vx[g], weights[par][...], preferred_element_type=F32
        )

    def ring_copy(c, k, way):
        return pltpu.make_async_remote_copy(
            src_ref=ring.at[c, k, way],
            dst_ref=ring.at[c, k + 1, way],
            send_sem=ring_send.at[c, k, way],
            recv_sem=ring_recv.at[c, k, way],
            device_id={"tp": (ahead, behind)[way]},
            device_id_type=MESH,
        )

    def z_copy(c):
        return pltpu.make_async_remote_copy(
            src_ref=ring.at[c, 3, 1 - z_lo],
            dst_ref=got_z.at[c],
            send_sem=z_send.at[c],
            recv_sem=z_recv.at[c],
            device_id={"tp": partner},
            device_id_type=MESH,
        )

    def share(c, k, way):
        owner = (y + 3 - k) % 4 if way == 0 else (y + 1 + k) % 4
        column = pl.multiple_of((way * 4 + owner) * WIDTH, HD)
        return jnp.dot(att[c], w[:, pl.ds(column, WIDTH)], preferred_element_type=F32)

    def finish(c):
        for h in range(HEADS):
            cols = pl.ds(h % 2 * CHUNK, CHUNK)
            part = acc[c, h // 2, :, cols]
            value = part[:HD] / part[HD : HD + 1]
            att[c, :, pl.ds(h * HD, HD)] = value.T.astype(BF16)
        for way in range(2):
            ring[c, 0, way] = share(c, 0, way).astype(BF16)
            ring_copy(c, 0, way).start()

    def pass_on(c, k):
        for way in range(2):
            mine = share(c, k, way)
            ring_copy(c, k - 1, way).wait_recv()
            ring[c, k, way] = (ring[c, k, way].astype(F32) + mine).astype(BF16)

            @pl.when(k < 3)
            def _():
                ring_copy(c, k, way).start()

        @pl.when(k == 3)
        def _():
            z_copy(c).start()

    def last(c):
        z_copy(c).wait_recv()
        total = ring[c, 3, z_lo].astype(F32) + got_z[c].astype(F32)
        rows[pl.ds(c * 4, 4)] = total.astype(BF16).reshape(4, PIECE, WIDTH)

    score(0, s0)

    def step(i, _):
        @pl.when(i == 1)
        def _():
            for part in range(2):
                arrived(8, part)
                pass_block(8, part)

        @pl.when(i == 3)
        def _():
            for part in range(2):
                arrived(6, part)
                pass_block(6, part)
            for part in range(2):
                arrived(5, part)
                arrived(7, part)

        @pl.when(i == 7)
        def _():
            load_w.wait()

        ready = pick(i, FINISH)

        @pl.when(ready >= 0)
        def _():
            finish(ready)

        move = pick(i, PASS_ON)

        @pl.when(move >= 0)
        def _():
            pass_on(move // 4, move % 4)

        done = pick(i, LAST)

        @pl.when(done >= 0)
        def _():
            last(done)

        @pl.when(i < TILES // 2)
        def _():
            score(2 * i + 1, s1)
            weigh(2 * i, 0)
            mix(jnp.maximum(2 * i - 1, 0), 1)
            score(jnp.minimum(2 * i + 2, TILES - 1), s0)
            weigh(2 * i + 1, 1)
            mix(2 * i, 0)

        @pl.when(i == TILES // 2)
        def _():
            mix(TILES - 1, 1)

        return 0

    lax.fori_loop(0, STEPS, step, 0)

    def parcel(k):
        return pltpu.make_async_remote_copy(
            src_ref=parcels.at[k],
            dst_ref=parcels_in.at[k],
            send_sem=parcel_send.at[k],
            recv_sem=parcel_recv.at[k],
            device_id={"seq": (s + k) % SEQ},
            device_id_type=MESH,
        )

    for k in range(1, SEQ):
        for r in range(2):
            parcels[k, r] = rows[out_from[(s + k) % SEQ * 2 + r]]
        parcel(k).start()
    for r in range(2):
        parcels_in[0, r] = rows[out_from[s * 2 + r]]
    for k in range(1, SEQ):
        parcel(k).wait_recv()
    for j in range(16):
        n = in_from[j]
        o_ref[pl.ds(j * PIECE, PIECE), :] = parcels_in[n // 2, n % 2]
    for k in range(1, SEQ):
        parcel(k).wait_send()

    for index in range(1, 4):
        for copy in copies(index, 1, 1, sibling):
            copy.wait_send()
    for i in range(4):
        for copy in copies(4 + i, 1, 1, sibling):
            copy.wait_send()
    for c in range(CHUNKS):
        for k in range(3):
            for way in range(2):
                ring_copy(c, k, way).wait_send()
        z_copy(c).wait_send()


def attention(queries, key_rows, value_rows, doc_lengths, piece_owner, out_weight):
    vmem = pl.BlockSpec(memory_space=pltpu.VMEM)
    return pl.pallas_call(
        attend_kernel,
        out_shape=jax.ShapeDtypeStruct((ROWS, WIDTH), BF16),
        in_specs=[
            vmem,
            vmem,
            vmem,
            pl.BlockSpec(memory_space=pltpu.SMEM),
            pl.BlockSpec(memory_space=pltpu.SMEM),
            pl.BlockSpec(memory_space=pl.ANY),
        ],
        out_specs=vmem,
        scratch_shapes=[
            pltpu.VMEM((CHUNKS, PAIRS, 2 * CHUNK, 2 * HD), BF16),
            pltpu.VMEM((ROWS, 2 * HD), BF16),
            pltpu.VMEM((HD + 16, ROWS), BF16),
            pltpu.VMEM((2, SPAN, 2 * HD), BF16),
            pltpu.VMEM((2, HD + 16, SPAN), BF16),
            pltpu.VMEM((CHUNKS, PAIRS, HD + 16, 2 * CHUNK), F32),
            pltpu.VMEM((CHUNKS, PAIRS, 8, 2 * CHUNK), F32),
            pltpu.VMEM((2, 8, 2 * CHUNK), F32),
            pltpu.VMEM((ROWS, 2 * CHUNK), I32),
            pltpu.VMEM((SPAN, 2 * CHUNK), F32),
            pltpu.VMEM((SPAN, 2 * CHUNK), F32),
            pltpu.VMEM((SPAN, 2 * CHUNK), BF16),
            pltpu.VMEM((SPAN, 2 * CHUNK), BF16),
            pltpu.VMEM((CHUNKS, CHUNK, HEADS * HD), BF16),
            pltpu.VMEM((HEADS * HD, 8 * WIDTH), BF16),
            pltpu.VMEM((CHUNKS, 4, 2, CHUNK, WIDTH), BF16),
            pltpu.VMEM((CHUNKS, CHUNK, WIDTH), BF16),
            pltpu.VMEM((16, PIECE, WIDTH), BF16),
            pltpu.VMEM((SEQ, 2, PIECE, WIDTH), BF16),
            pltpu.VMEM((SEQ, 2, PIECE, WIDTH), BF16),
            pltpu.SMEM((2 * SEQ,), I32),
            pltpu.SMEM((16,), I32),
            pltpu.SemaphoreType.DMA((8, 2)),
            pltpu.SemaphoreType.DMA((BACK + 1, 2)),
            pltpu.SemaphoreType.DMA,
            pltpu.SemaphoreType.DMA((CHUNKS, 3, 2)),
            pltpu.SemaphoreType.DMA((CHUNKS, 3, 2)),
            pltpu.SemaphoreType.DMA((CHUNKS,)),
            pltpu.SemaphoreType.DMA((CHUNKS,)),
            pltpu.SemaphoreType.DMA((SEQ,)),
            pltpu.SemaphoreType.DMA((SEQ,)),
        ],
        compiler_params=pltpu.CompilerParams(
            collective_id=0, has_side_effects=True, vmem_limit_bytes=56 << 20
        ),
    )(queries, key_rows, value_rows, doc_lengths, piece_owner, out_weight)


def on_device(queries, key_heads, value_heads, out_weight, doc_lengths, piece_owner):
    return attention(
        queries.reshape(ROWS, HEADS * HD),
        key_heads.reshape(ROWS, HD),
        value_heads.reshape(ROWS, HD),
        doc_lengths,
        piece_owner,
        out_weight,
    )


def solution(mesh):
    placed = (
        P("seq", "tp", None),
        P("seq", "tp", None),
        P("seq", "tp", None),
        P("tp", None),
        P(),
        P(),
    )
    return jax.shard_map(
        on_device, mesh=mesh, in_specs=placed, out_specs=P("seq", "tp"), check_vma=False
    )
```

time: 133 us -> 117 us (0.88)
  waiting for transfers between devices: 18.8 us -> 0 us
  Pallas kernels: 97.5 us -> 112 us
  starting transfers between devices: 6.88 us -> 0 us
  other arithmetic: 2.05 us -> 0 us
  local copies, waits for them, and re-layouts: 6.47 us -> 4.47 us
    all_to_all x1 -> x0, waiting for transfers between devices: 18.8 us -> none  [route(): lax.all_to_all(rows, 'seq', split_axis=0, concat_axis=0, tiled=True)]
    pallas_call x1, Pallas kernels: 97.5 us -> 112 us  [attention(): pl.pallas_call(attend_kernel, out_shape=jax.ShapeDtypeStruct((ROWS, WIDTH...]
    all_to_all x1 -> x0, starting transfers between devices: 6.88 us -> none  [route(): lax.all_to_all(rows, 'seq', split_axis=0, concat_axis=0, tiled=True)]
    unnamed x3 -> x2, local copies, waits for them, and re-layouts: 2.5 us -> 4.47 us
    all_to_all x1 -> x0, local copies, waits for them, and re-layouts: 1.49 us -> none  [route(): lax.all_to_all(rows, 'seq', split_axis=0, concat_axis=0, tiled=True)]
    reshape x1 -> x0, local copies, waits for them, and re-layouts: 1.39 us -> none  [route(): stacked = row_data.reshape(pieces, piece_len * row_width)]
  transfers between devices with their start and end apart: 1 -> 0, of which waited for: 1 -> 0; matrix products, arithmetic and copies ran while one was open for 1% -> 0% of each run, Pallas kernels for 0% -> 0%
where the time goes in v3:
time: 117 us
  Pallas kernels  112 us (96%)
  local copies, waits for them, and re-layouts  4.47 us (4%)
    pallas_call x1, Pallas kernels, attention(): pl.pallas_call(attend_kernel, out_shape=jax.ShapeDtypeStruct((ROWS, WIDTH...  112 us
    unnamed x2, local copies, waits for them, and re-layouts  4.47 us

profile of v3, /device:TPU:1, one launch (start us, length us, event | category | flops | bytes accessed | tf_op | source)
XLA Modules:
  0.0 116.8 jit_solution(7290779051227197728)
XLA Ops:
  0.0 2.5 %copy.9 = bf16[64,8,8,128]{3,1,2,0:T(8,128)(2,1)} copy(bf16[64,8,8,128]{3,2,1,0:T(8,128)(2,1)} %bitcast.7) | data formatting | bytes 2097152
  2.5 112.3 %shard_map.64 = bf16[512,640]{1,0:T(8,128)(2,1)} custom-call(bf16[512,1024]{1,0:T(8,128)(2,1)} %bitcast.6, bf16[512,128]{1,0:T(8,128)(2,1)} %bitcast.8, bf16[512,128]{1,0:T(8,128)(2,1)} %bitcast.9, s32[4]{0:T(128)} %len_ref.1, s32[256]{0:T(256)} %owner_ref.1, bf16[1024,5120]{1,0:T(8,128)(2,1)} %w_hbm.1), custom_call_target="tpu_custom_call" | custom-call | tf_op jit(solution)/shard_map/pallas_call | solution.py:432
  114.8 2.0 %copy.11 = bf16[512,640]{1,0:T(8,128)(2,1)} copy(bf16[512,640]{1,0:T(8,128)(2,1)} %shard_map.64) | data formatting | bytes 1310720

commit v4 on v3

--- a/solution.py
+++ b/solution.py
@@ -22,10 +22,17 @@
 PIECE = 32
 SEQ = 16
 TILES = 2 * CHUNKS * PAIRS
-FINISH = {7: 0, 9: 1, 13: 2, 17: 3}
-PASS_ON = {9: 1, 11: 2, 13: 5, 15: 3, 16: 6, 18: 9, 19: 7, 20: 13, 21: 10, 22: 14, 23: 11, 24: 15}
-LAST = {17: 0, 21: 1, 24: 2, 25: 3}
-STEPS = 26
+SLICES = ((0, 384), (384, 256))
+FINISH = {5: 0, 9: 1, 13: 2, 17: 3}
+PASS_ON = (
+    {5: 4, 7: 1, 8: 5, 9: 2, 11: 9, 12: 3, 13: 7, 14: 17, 16: 11, 17: 14, 18: 18, 19: 21, 20: 25, 21: 15, 22: 28, 23: 19, 24: 22, 25: 26, 26: 29, 27: 23, 28: 27, 29: 30, 30: 31},
+    {9: 6, 13: 10, 14: 20},
+    {9: 12, 13: 13},
+)
+LAST = {13: 0, 15: 1, 20: 2, 25: 3, 26: 4, 30: 5, 31: 6, 32: 7}
+ROUTE = {31: 0, 32: 1}
+PLACES = 15
+STEPS = 33
 SCORE = HD**-0.5 * 1.4426950408889634
 MESH = pl.DeviceIdType.MESH
 
@@ -65,10 +72,17 @@
 
 def attend_kernel(
     q_ref, k_ref, v_ref, len_ref, owner_ref, w_hbm, o_ref,
-    qx, k_own, v_own, kx, vx, acc, top, fac, diff, s0, s1, p0, p1, att, w, ring, got_z,
-    rows, parcels, parcels_in, out_from, in_from,
+    qx, k_own, v_own, kx, vx, acc, top, fac, diff, s0, s1, p0, p1, att, w, parts,
+    ring0, ring1, got0, got1, rows0, rows1, parcels0, parcels1, in0, in1, out_from, in_from,
     send, recv, w_sem, ring_send, ring_recv, z_send, z_recv, parcel_send, parcel_recv,
 ):
+    ring, got_z, rows, parcels, parcels_in = (
+        (ring0, ring1),
+        (got0, got1),
+        (rows0, rows1),
+        (parcels0, parcels1),
+        (in0, in1),
+    )
     s, z, core, at = places()
     t = lax.axis_index("tp")
     z_lo, y = t // 4, t % 4
@@ -152,6 +166,9 @@
         def _():
             go(4, None, 1, sibling, part)
 
+    for part in range(2):
+        go(1, None, 8, far_x, part)
+
     ends = []
     total = 0
     for d in range(4):
@@ -164,22 +181,13 @@
         for c in range(CHUNKS):
             queries = pl.ds(c * CHUNK, CHUNK)
             side = pl.ds(h % 2 * CHUNK, CHUNK)
-            qx[c, h // 2, side, :HD] = q_ref[queries, pl.ds(h * HD, HD)]
+            qx[c, h // 2, side, :HD] = q_ref[queries, h, :]
             qx[c, h // 2, side, HD:] = mine[c * CHUNK : (c + 1) * CHUNK]
 
     own_seen = doc_of(ends, row + s * ROWS) == lane
     k_own[:, HD:] = jnp.where(own_seen, 0.0, 1.0).astype(BF16)
     v_own[HD:] = jnp.ones((16, ROWS), BF16)
 
-    def mark(delta, _):
-        start = pl.multiple_of((delta - 1) % GROUP * ROWS, ROWS)
-        seen = doc_of(ends, row + (s - delta) * ROWS) == lane
-        kx[(delta - 1) // GROUP, pl.ds(start, ROWS), HD:] = jnp.where(seen, 0.0, 1.0).astype(BF16)
-        return 0
-
-    lax.fori_loop(1, BACK + 1, mark, 0)
-    for g in range(2):
-        vx[g, HD:, :] = jnp.ones((16, SPAN), BF16)
     diff[...] = lax.broadcasted_iota(I32, (ROWS, 2 * CHUNK), 0) - (
         lax.broadcasted_iota(I32, (ROWS, 2 * CHUNK), 1) % CHUNK
     )
@@ -216,49 +224,26 @@
 
     lax.fori_loop(0, 2 * CHUNKS, own_pass, 0)
 
-    for part in range(2):
-        copy_of(0, None, 4, next_x, part).wait_send()
-        go(1, None, 8, far_x, part)
-
-    own = [owner_ref[s * 16 + k] for k in range(16)]
-    place = []
-    for k in range(16):
-        rank = 0
-        for j in range(k):
-            rank = rank + jnp.where(own[j] == own[k], 1, 0)
-        place.append(2 * own[k] + rank)
-    for n in range(2 * SEQ):
-        piece = 0
-        for k in range(16):
-            piece = piece + jnp.where(place[k] == n, k, 0)
-        out_from[n] = piece
-    before = 0
-    found = [0] * 16
-    for source in range(SEQ):
-        count = 0
-        for k in range(16):
-            count = count + jnp.where(owner_ref[source * 16 + k] == s, 1, 0)
-        far = (s - source + SEQ) % SEQ
-        for j in range(16):
-            for r in range(2):
-                hit = (before + r == j) & (r < count)
-                found[j] = found[j] + jnp.where(hit, 2 * far + r, 0)
-        before = before + count
-    for j in range(16):
-        in_from[j] = found[j]
-
-    for part in range(2):
-        arrived(2, part)
-        pass_block(2, part)
+    def mark(delta, _):
+        start = pl.multiple_of((delta - 1) % GROUP * ROWS, ROWS)
+        seen = doc_of(ends, row + (s - delta) * ROWS) == lane
+        kx[(delta - 1) // GROUP, pl.ds(start, ROWS), HD:] = jnp.where(seen, 0.0, 1.0).astype(BF16)
+        return 0
+
+    lax.fori_loop(1, BACK + 1, mark, 0)
+    for g in range(2):
+        vx[g, HD:, :] = jnp.ones((16, SPAN), BF16)
+    for name in (2, 8):
+        for part in range(2):
+            arrived(name, part)
+            pass_block(name, part)
     for part in range(2):
         arrived(1, part)
         arrived(3, part)
 
     def tile(n):
         b = n // PAIRS
-        c = jnp.where(b < 4, b % 2, b // 2)
-        g = jnp.where(b < 4, b // 2, b % 2)
-        return c, g, n % PAIRS
+        return b // 2, b % 2, n % PAIRS
 
     def score(n, out):
         c, g, p = tile(n)
@@ -279,22 +264,22 @@
             vx[g], weights[par][...], preferred_element_type=F32
         )
 
-    def ring_copy(c, k, way):
+    def ring_copy(j, c, k, way):
         return pltpu.make_async_remote_copy(
-            src_ref=ring.at[c, k, way],
-            dst_ref=ring.at[c, k + 1, way],
-            send_sem=ring_send.at[c, k, way],
-            recv_sem=ring_recv.at[c, k, way],
+            src_ref=ring[j].at[c, k, way],
+            dst_ref=ring[j].at[c, k + 1, way],
+            send_sem=ring_send.at[j, c, k, way],
+            recv_sem=ring_recv.at[j, c, k, way],
             device_id={"tp": (ahead, behind)[way]},
             device_id_type=MESH,
         )
 
-    def z_copy(c):
+    def z_copy(j, c):
         return pltpu.make_async_remote_copy(
-            src_ref=ring.at[c, 3, 1 - z_lo],
-            dst_ref=got_z.at[c],
-            send_sem=z_send.at[c],
-            recv_sem=z_recv.at[c],
+            src_ref=ring[j].at[c, 3, 1 - z_lo],
+            dst_ref=got_z[j].at[c],
+            send_sem=z_send.at[j, c],
+            recv_sem=z_recv.at[j, c],
             device_id={"tp": partner},
             device_id_type=MESH,
         )
@@ -311,38 +296,64 @@
             value = part[:HD] / part[HD : HD + 1]
             att[c, :, pl.ds(h * HD, HD)] = value.T.astype(BF16)
         for way in range(2):
-            ring[c, 0, way] = share(c, 0, way).astype(BF16)
-            ring_copy(c, 0, way).start()
-
-    def pass_on(c, k):
-        for way in range(2):
-            mine = share(c, k, way)
-            ring_copy(c, k - 1, way).wait_recv()
-            ring[c, k, way] = (ring[c, k, way].astype(F32) + mine).astype(BF16)
-
-            @pl.when(k < 3)
-            def _():
-                ring_copy(c, k, way).start()
+            first = share(c, 0, way).astype(BF16)
+            for j, (column, width) in enumerate(SLICES):
+                ring[j][c, 0, way] = first[:, column : column + width]
+            ring_copy(0, c, 0, way).start()
+
+        def others(k, _):
+            for way in range(2):
+                parts[c, k - 1, way] = share(c, k, way)
+            return 0
+
+        lax.fori_loop(1, 4, others, 0)
+
+    def pass_on(j, c, k):
+        column, width = SLICES[j]
+
+        @pl.when(k > 0)
+        def _():
+            for way in range(2):
+                ring_copy(j, c, k - 1, way).wait_recv()
+                mine = parts[c, k - 1, way, :, column : column + width]
+                ring[j][c, k, way] = (ring[j][c, k, way].astype(F32) + mine).astype(BF16)
+
+        @pl.when(k < 3)
+        def _():
+            for way in range(2):
+                ring_copy(j, c, k, way).start()
 
         @pl.when(k == 3)
         def _():
-            z_copy(c).start()
-
-    def last(c):
-        z_copy(c).wait_recv()
-        total = ring[c, 3, z_lo].astype(F32) + got_z[c].astype(F32)
-        rows[pl.ds(c * 4, 4)] = total.astype(BF16).reshape(4, PIECE, WIDTH)
+            z_copy(j, c).start()
+
+    def last(j, c):
+        z_copy(j, c).wait_recv()
+        total = ring[j][c, 3, z_lo].astype(F32) + got_z[j][c].astype(F32)
+        rows[j][pl.ds(c * 4, 4)] = total.astype(BF16).reshape(4, PIECE, SLICES[j][1])
+
+    def parcel(j, k):
+        return pltpu.make_async_remote_copy(
+            src_ref=parcels[j].at[k],
+            dst_ref=parcels_in[j].at[k],
+            send_sem=parcel_send.at[j, k],
+            recv_sem=parcel_recv.at[j, k],
+            device_id={"seq": (s + k) % SEQ},
+            device_id_type=MESH,
+        )
+
+    def route(j):
+        for k in range(1, SEQ):
+            for r in range(2):
+                parcels[j][k, r] = rows[j][out_from[(s + k) % SEQ * 2 + r]]
+            parcel(j, k).start()
+        for r in range(2):
+            parcels_in[j][0, r] = rows[j][out_from[s * 2 + r]]
 
     score(0, s0)
 
     def step(i, _):
         @pl.when(i == 1)
-        def _():
-            for part in range(2):
-                arrived(8, part)
-                pass_block(8, part)
-
-        @pl.when(i == 3)
         def _():
             for part in range(2):
                 arrived(6, part)
@@ -351,27 +362,64 @@
                 arrived(5, part)
                 arrived(7, part)
 
-        @pl.when(i == 7)
+        @pl.when(i == 5)
         def _():
             load_w.wait()
 
+        @pl.when(i == PLACES)
+        def _():
+            own = [owner_ref[s * 16 + k] for k in range(16)]
+            place = []
+            for k in range(16):
+                rank = 0
+                for j in range(k):
+                    rank = rank + jnp.where(own[j] == own[k], 1, 0)
+                place.append(2 * own[k] + rank)
+            for n in range(2 * SEQ):
+                piece = 0
+                for k in range(16):
+                    piece = piece + jnp.where(place[k] == n, k, 0)
+                out_from[n] = piece
+            before = 0
+            found = [0] * 16
+            for source in range(SEQ):
+                count = 0
+                for k in range(16):
+                    count = count + jnp.where(owner_ref[source * 16 + k] == s, 1, 0)
+                far = (s - source + SEQ) % SEQ
+                for j in range(16):
+                    for r in range(2):
+                        hit = (before + r == j) & (r < count)
+                        found[j] = found[j] + jnp.where(hit, 2 * far + r, 0)
+                before = before + count
+            for j in range(16):
+                in_from[j] = found[j]
+
         ready = pick(i, FINISH)
 
         @pl.when(ready >= 0)
         def _():
             finish(ready)
 
-        move = pick(i, PASS_ON)
-
-        @pl.when(move >= 0)
-        def _():
-            pass_on(move // 4, move % 4)
+        for table in PASS_ON:
+            move = pick(i, table)
+            for j in range(2):
+
+                @pl.when((move >= 0) & (move // 4 % 2 == j))
+                def _(j=j):
+                    pass_on(j, move // 8, move % 4)
 
         done = pick(i, LAST)
-
-        @pl.when(done >= 0)
-        def _():
-            last(done)
+        leave = pick(i, ROUTE)
+        for j in range(2):
+
+            @pl.when((done >= 0) & (done % 2 == j))
+            def _(j=j):
+                last(j, done // 2)
+
+            @pl.when(leave == j)
+            def _(j=j):
+                route(j)
 
         @pl.when(i < TILES // 2)
         def _():
@@ -390,41 +438,28 @@
 
     lax.fori_loop(0, STEPS, step, 0)
 
-    def parcel(k):
-        return pltpu.make_async_remote_copy(
-            src_ref=parcels.at[k],
-            dst_ref=parcels_in.at[k],
-            send_sem=parcel_send.at[k],
-            recv_sem=parcel_recv.at[k],
-            device_id={"seq": (s + k) % SEQ},
-            device_id_type=MESH,
-        )
-
-    for k in range(1, SEQ):
-        for r in range(2):
-            parcels[k, r] = rows[out_from[(s + k) % SEQ * 2 + r]]
-        parcel(k).start()
-    for r in range(2):
-        parcels_in[0, r] = rows[out_from[s * 2 + r]]
-    for k in range(1, SEQ):
-        parcel(k).wait_recv()
-    for j in range(16):
-        n = in_from[j]
-        o_ref[pl.ds(j * PIECE, PIECE), :] = parcels_in[n // 2, n % 2]
-    for k in range(1, SEQ):
-        parcel(k).wait_send()
-
-    for index in range(1, 4):
+    for j, (column, width) in enumerate(SLICES):
+        for k in range(1, SEQ):
+            parcel(j, k).wait_recv()
+        for k in range(16):
+            n = in_from[k]
+            o_ref[pl.ds(k * PIECE, PIECE), column : column + width] = parcels_in[j][n // 2, n % 2]
+    for j in range(2):
+        for k in range(1, SEQ):
+            parcel(j, k).wait_send()
+
+    for index in range(4):
         for copy in copies(index, 1, 1, sibling):
             copy.wait_send()
     for i in range(4):
         for copy in copies(4 + i, 1, 1, sibling):
             copy.wait_send()
-    for c in range(CHUNKS):
-        for k in range(3):
-            for way in range(2):
-                ring_copy(c, k, way).wait_send()
-        z_copy(c).wait_send()
+    for j in range(2):
+        for c in range(CHUNKS):
+            for k in range(3):
+                for way in range(2):
+                    ring_copy(j, c, k, way).wait_send()
+            z_copy(j, c).wait_send()
 
 
 def attention(queries, key_rows, value_rows, doc_lengths, piece_owner, out_weight):
@@ -457,22 +492,23 @@
             pltpu.VMEM((SPAN, 2 * CHUNK), BF16),
             pltpu.VMEM((CHUNKS, CHUNK, HEADS * HD), BF16),
             pltpu.VMEM((HEADS * HD, 8 * WIDTH), BF16),
-            pltpu.VMEM((CHUNKS, 4, 2, CHUNK, WIDTH), BF16),
-            pltpu.VMEM((CHUNKS, CHUNK, WIDTH), BF16),
-            pltpu.VMEM((16, PIECE, WIDTH), BF16),
-            pltpu.VMEM((SEQ, 2, PIECE, WIDTH), BF16),
-            pltpu.VMEM((SEQ, 2, PIECE, WIDTH), BF16),
+            pltpu.VMEM((CHUNKS, 3, 2, CHUNK, WIDTH), F32),
+            *(pltpu.VMEM((CHUNKS, 4, 2, CHUNK, width), BF16) for _, width in SLICES),
+            *(pltpu.VMEM((CHUNKS, CHUNK, width), BF16) for _, width in SLICES),
+            *(pltpu.VMEM((16, PIECE, width), BF16) for _, width in SLICES),
+            *(pltpu.VMEM((SEQ, 2, PIECE, width), BF16) for _, width in SLICES),
+            *(pltpu.VMEM((SEQ, 2, PIECE, width), BF16) for _, width in SLICES),
             pltpu.SMEM((2 * SEQ,), I32),
             pltpu.SMEM((16,), I32),
             pltpu.SemaphoreType.DMA((8, 2)),
             pltpu.SemaphoreType.DMA((BACK + 1, 2)),
             pltpu.SemaphoreType.DMA,
-            pltpu.SemaphoreType.DMA((CHUNKS, 3, 2)),
-            pltpu.SemaphoreType.DMA((CHUNKS, 3, 2)),
-            pltpu.SemaphoreType.DMA((CHUNKS,)),
-            pltpu.SemaphoreType.DMA((CHUNKS,)),
-            pltpu.SemaphoreType.DMA((SEQ,)),
-            pltpu.SemaphoreType.DMA((SEQ,)),
+            pltpu.SemaphoreType.DMA((2, CHUNKS, 3, 2)),
+            pltpu.SemaphoreType.DMA((2, CHUNKS, 3, 2)),
+            pltpu.SemaphoreType.DMA((2, CHUNKS)),
+            pltpu.SemaphoreType.DMA((2, CHUNKS)),
+            pltpu.SemaphoreType.DMA((2, SEQ)),
+            pltpu.SemaphoreType.DMA((2, SEQ)),
         ],
         compiler_params=pltpu.CompilerParams(
             collective_id=0, has_side_effects=True, vmem_limit_bytes=56 << 20
@@ -482,7 +518,7 @@
 
 def on_device(queries, key_heads, value_heads, out_weight, doc_lengths, piece_owner):
     return attention(
-        queries.reshape(ROWS, HEADS * HD),
+        queries,
         key_heads.reshape(ROWS, HD),
         value_heads.reshape(ROWS, HD),
         doc_lengths,

time: 117 us -> 109 us (0.932)
  Pallas kernels: 112 us -> 106 us
  local copies, waits for them, and re-layouts: 4.47 us -> 1.98 us
    pallas_call x1, Pallas kernels: 112 us -> 106 us  [attention(): pl.pallas_call(attend_kernel, out_shape=jax.ShapeDtypeStruct((ROWS, WIDTH...]
    unnamed x2 -> x1, local copies, waits for them, and re-layouts: 4.47 us -> 1.98 us
where the time goes in v4:
time: 109 us; the launch traced here: 108 us
  Pallas kernels  106 us (97%)
  local copies, waits for them, and re-layouts  1.98 us (2%)
    pallas_call x1, Pallas kernels, attention(): pl.pallas_call(attend_kernel, out_shape=jax.ShapeDtypeStruct((ROWS, WIDTH...  106 us

profile of v4, /device:TPU:1, one launch (start us, length us, event | category | flops | bytes accessed | tf_op | source)
XLA Modules:
  0.0 108.4 jit_solution(6098423267482450859)
XLA Ops:
  0.0 106.5 %shard_map.64 = bf16[512,640]{1,0:T(8,128)(2,1)} custom-call(bf16[512,8,128]{2,1,0:T(8,128)(2,1)} %q_ref.1, bf16[512,128]{1,0:T(8,128)(2,1)} %bitcast.2, bf16[512,128]{1,0:T(8,128)(2,1)} %bitcast.3, s32[4]{0:T(128)} %len_ref.1, s32[256]{0:T(256)} %owner_ref.1, bf16[1024,5120]{1,0:T(8,128)(2,1)} %w_hbm.1), custom_call_target="tpu_custom_call" | custom-call | tf_op jit(solution)/shard_map/pallas_call | solution.py:467
  106.5 2.0 %copy.8 = bf16[512,640]{1,0:T(8,128)(2,1)} copy(bf16[512,640]{1,0:T(8,128)(2,1)} %shard_map.64) | data formatting | bytes 1310720

commit v5 on v4

--- a/solution.py
+++ b/solution.py
@@ -22,17 +22,19 @@
 PIECE = 32
 SEQ = 16
 TILES = 2 * CHUNKS * PAIRS
-SLICES = ((0, 384), (384, 256))
+SLICES = ((0, 256), (256, 256), (512, 128))
+PARTS = len(SLICES)
+LATE = ((2, 2), (3, 2))
 FINISH = {5: 0, 9: 1, 13: 2, 17: 3}
+SHARE = {6: 1, 7: 2, 8: 3, 10: 5, 11: 6, 12: 7, 14: 9, 15: 10, 16: 11, 18: 13, 19: 14, 20: 15}
 PASS_ON = (
-    {5: 4, 7: 1, 8: 5, 9: 2, 11: 9, 12: 3, 13: 7, 14: 17, 16: 11, 17: 14, 18: 18, 19: 21, 20: 25, 21: 15, 22: 28, 23: 19, 24: 22, 25: 26, 26: 29, 27: 23, 28: 27, 29: 30, 30: 31},
-    {9: 6, 13: 10, 14: 20},
-    {9: 12, 13: 13},
+    {7: 1, 8: 5, 9: 2, 10: 6, 11: 13, 12: 17, 13: 7, 14: 14, 15: 25, 16: 15, 17: 19, 18: 32, 19: 30, 21: 37, 22: 41, 23: 27, 24: 33, 25: 45, 26: 31, 27: 23, 28: 38, 29: 42, 30: 34, 31: 46, 32: 39, 33: 43, 34: 35, 35: 47},
+    {8: 9, 10: 10, 12: 3, 13: 11, 14: 18, 15: 29, 16: 21, 17: 26, 18: 44, 19: 22},
 )
-LAST = {13: 0, 15: 1, 20: 2, 25: 3, 26: 4, 30: 5, 31: 6, 32: 7}
-ROUTE = {31: 0, 32: 1}
+LAST = {14: 0, 15: 1, 16: 2, 20: 3, 22: 4, 28: 6, 30: 7, 31: 5, 35: 9, 36: 10, 37: 8, 38: 11}
+ROUTE = {35: 0, 36: 1, 38: 2}
 PLACES = 15
-STEPS = 33
+STEPS = 39
 SCORE = HD**-0.5 * 1.4426950408889634
 MESH = pl.DeviceIdType.MESH
 
@@ -70,18 +72,30 @@
     return found
 
 
+def one_of(chunk, units):
+    found = chunk == units[0][0]
+    for unit in units[1:]:
+        found = found | (chunk == unit[0])
+    return found
+
+
 def attend_kernel(
     q_ref, k_ref, v_ref, len_ref, owner_ref, w_hbm, o_ref,
     qx, k_own, v_own, kx, vx, acc, top, fac, diff, s0, s1, p0, p1, att, w, parts,
-    ring0, ring1, got0, got1, rows0, rows1, parcels0, parcels1, in0, in1, out_from, in_from,
+    ring0, ring1, ring2,
+    got0, got1, got2,
+    rows0, rows1, rows2,
+    parcels0, parcels1, parcels2,
+    in0, in1, in2,
+    out_from, in_from,
     send, recv, w_sem, ring_send, ring_recv, z_send, z_recv, parcel_send, parcel_recv,
 ):
     ring, got_z, rows, parcels, parcels_in = (
-        (ring0, ring1),
-        (got0, got1),
-        (rows0, rows1),
-        (parcels0, parcels1),
-        (in0, in1),
+        (ring0, ring1, ring2),
+        (got0, got1, got2),
+        (rows0, rows1, rows2),
+        (parcels0, parcels1, parcels2),
+        (in0, in1, in2),
     )
     s, z, core, at = places()
     t = lax.axis_index("tp")
@@ -299,14 +313,18 @@
             first = share(c, 0, way).astype(BF16)
             for j, (column, width) in enumerate(SLICES):
                 ring[j][c, 0, way] = first[:, column : column + width]
-            ring_copy(0, c, 0, way).start()
-
-        def others(k, _):
-            for way in range(2):
-                parts[c, k - 1, way] = share(c, k, way)
-            return 0
-
-        lax.fori_loop(1, 4, others, 0)
+            for j in range(PARTS):
+                later = [u for u in LATE if u[1] == j]
+                if later:
+                    pl.when(jnp.logical_not(one_of(c, later)))(
+                        lambda j=j, way=way: ring_copy(j, c, 0, way).start()
+                    )
+                else:
+                    ring_copy(j, c, 0, way).start()
+
+    def compute_shares(c, k):
+        for way in range(2):
+            parts[c, k - 1, way] = share(c, k, way)
 
     def pass_on(j, c, k):
         column, width = SLICES[j]
@@ -401,21 +419,27 @@
         def _():
             finish(ready)
 
+        shares = pick(i, SHARE)
+
+        @pl.when(shares >= 0)
+        def _():
+            compute_shares(shares // 4, shares % 4)
+
         for table in PASS_ON:
             move = pick(i, table)
-            for j in range(2):
-
-                @pl.when((move >= 0) & (move // 4 % 2 == j))
+            for j in range(PARTS):
+
+                @pl.when((move >= 0) & (move // 4 % PARTS == j))
                 def _(j=j):
-                    pass_on(j, move // 8, move % 4)
+                    pass_on(j, move // (4 * PARTS), move % 4)
 
         done = pick(i, LAST)
         leave = pick(i, ROUTE)
-        for j in range(2):
-
-            @pl.when((done >= 0) & (done % 2 == j))
+        for j in range(PARTS):
+
+            @pl.when((done >= 0) & (done % PARTS == j))
             def _(j=j):
-                last(j, done // 2)
+                last(j, done // PARTS)
 
             @pl.when(leave == j)
             def _(j=j):
@@ -444,7 +468,7 @@
         for k in range(16):
             n = in_from[k]
             o_ref[pl.ds(k * PIECE, PIECE), column : column + width] = parcels_in[j][n // 2, n % 2]
-    for j in range(2):
+    for j in range(PARTS):
         for k in range(1, SEQ):
             parcel(j, k).wait_send()
 
@@ -454,7 +478,7 @@
     for i in range(4):
         for copy in copies(4 + i, 1, 1, sibling):
             copy.wait_send()
-    for j in range(2):
+    for j in range(PARTS):
         for c in range(CHUNKS):
             for k in range(3):
                 for way in range(2):
@@ -503,12 +527,12 @@
             pltpu.SemaphoreType.DMA((8, 2)),
             pltpu.SemaphoreType.DMA((BACK + 1, 2)),
             pltpu.SemaphoreType.DMA,
-            pltpu.SemaphoreType.DMA((2, CHUNKS, 3, 2)),
-            pltpu.SemaphoreType.DMA((2, CHUNKS, 3, 2)),
-            pltpu.SemaphoreType.DMA((2, CHUNKS)),
-            pltpu.SemaphoreType.DMA((2, CHUNKS)),
-            pltpu.SemaphoreType.DMA((2, SEQ)),
-            pltpu.SemaphoreType.DMA((2, SEQ)),
+            pltpu.SemaphoreType.DMA((PARTS, CHUNKS, 3, 2)),
+            pltpu.SemaphoreType.DMA((PARTS, CHUNKS, 3, 2)),
+            pltpu.SemaphoreType.DMA((PARTS, CHUNKS)),
+            pltpu.SemaphoreType.DMA((PARTS, CHUNKS)),
+            pltpu.SemaphoreType.DMA((PARTS, SEQ)),
+            pltpu.SemaphoreType.DMA((PARTS, SEQ)),
         ],
         compiler_params=pltpu.CompilerParams(
             collective_id=0, has_side_effects=True, vmem_limit_bytes=56 << 20

time: 109 us -> 107 us (0.982)
    pallas_call x1, Pallas kernels: 106 us -> 105 us  [attention(): pl.pallas_call(attend_kernel, out_shape=jax.ShapeDtypeStruct((ROWS, WIDTH...]
where the time goes in v5:
time: 107 us
  Pallas kernels  105 us (98%)
  local copies, waits for them, and re-layouts  1.98 us (2%)
    pallas_call x1, Pallas kernels, attention(): pl.pallas_call(attend_kernel, out_shape=jax.ShapeDtypeStruct((ROWS, WIDTH...  105 us

profile of v5, /device:TPU:1, one launch (start us, length us, event | category | flops | bytes accessed | tf_op | source)
XLA Modules:
  0.0 106.9 jit_solution(13122283327267152351)
XLA Ops:
  0.0 104.9 %shard_map.64 = bf16[512,640]{1,0:T(8,128)(2,1)} custom-call(bf16[512,8,128]{2,1,0:T(8,128)(2,1)} %q_ref.1, bf16[512,128]{1,0:T(8,128)(2,1)} %bitcast.2, bf16[512,128]{1,0:T(8,128)(2,1)} %bitcast.3, s32[4]{0:T(128)} %len_ref.1, s32[256]{0:T(256)} %owner_ref.1, bf16[1024,5120]{1,0:T(8,128)(2,1)} %w_hbm.1), custom_call_target="tpu_custom_call" | custom-call | tf_op jit(solution)/shard_map/pallas_call | solution.py:491
  104.9 2.0 %copy.8 = bf16[512,640]{1,0:T(8,128)(2,1)} copy(bf16[512,640]{1,0:T(8,128)(2,1)} %shard_map.64) | data formatting | bytes 1310720

commit v6 on v5

--- a/solution.py
+++ b/solution.py
@@ -24,17 +24,17 @@
 TILES = 2 * CHUNKS * PAIRS
 SLICES = ((0, 256), (256, 256), (512, 128))
 PARTS = len(SLICES)
-LATE = ((2, 2), (3, 2))
+LATE = ((1, 2), (2, 2), (3, 2))
 FINISH = {5: 0, 9: 1, 13: 2, 17: 3}
 SHARE = {6: 1, 7: 2, 8: 3, 10: 5, 11: 6, 12: 7, 14: 9, 15: 10, 16: 11, 18: 13, 19: 14, 20: 15}
 PASS_ON = (
-    {7: 1, 8: 5, 9: 2, 10: 6, 11: 13, 12: 17, 13: 7, 14: 14, 15: 25, 16: 15, 17: 19, 18: 32, 19: 30, 21: 37, 22: 41, 23: 27, 24: 33, 25: 45, 26: 31, 27: 23, 28: 38, 29: 42, 30: 34, 31: 46, 32: 39, 33: 43, 34: 35, 35: 47},
-    {8: 9, 10: 10, 12: 3, 13: 11, 14: 18, 15: 29, 16: 21, 17: 26, 18: 44, 19: 22},
+    {7: 1, 8: 5, 9: 2, 10: 6, 11: 13, 12: 3, 13: 7, 14: 14, 15: 25, 16: 15, 17: 19, 18: 32, 19: 30, 21: 37, 22: 41, 23: 27, 24: 33, 25: 45, 26: 31, 27: 38, 28: 42, 29: 34, 30: 46, 31: 39, 32: 43, 33: 35, 34: 47},
+    {8: 9, 9: 20, 10: 10, 11: 17, 12: 21, 13: 11, 14: 18, 15: 29, 16: 22, 17: 26, 18: 44, 19: 23},
 )
-LAST = {14: 0, 15: 1, 16: 2, 20: 3, 22: 4, 28: 6, 30: 7, 31: 5, 35: 9, 36: 10, 37: 8, 38: 11}
-ROUTE = {35: 0, 36: 1, 38: 2}
+LAST = {14: 0, 15: 1, 16: 2, 20: 3, 22: 4, 23: 5, 27: 6, 30: 7, 34: 9, 35: 10, 36: 8, 37: 11}
+ROUTE = {34: 0, 35: 1, 37: 2}
 PLACES = 15
-STEPS = 39
+STEPS = 38
 SCORE = HD**-0.5 * 1.4426950408889634
 MESH = pl.DeviceIdType.MESH
 

time: 107 us -> 106 us (level)
  no operation moved by 1% of the time
where the time goes in v6:
time: 106 us
  Pallas kernels  104 us (98%)
  local copies, waits for them, and re-layouts  1.98 us (2%)
    pallas_call x1, Pallas kernels, attention(): pl.pallas_call(attend_kernel, out_shape=jax.ShapeDtypeStruct((ROWS, WIDTH...  104 us

profile of v6, /device:TPU:1, one launch (start us, length us, event | category | flops | bytes accessed | tf_op | source)
XLA Modules:
  0.0 106.2 jit_solution(16479802751953929216)
XLA Ops:
  0.0 104.2 %shard_map.64 = bf16[512,640]{1,0:T(8,128)(2,1)} custom-call(bf16[512,8,128]{2,1,0:T(8,128)(2,1)} %q_ref.1, bf16[512,128]{1,0:T(8,128)(2,1)} %bitcast.2, bf16[512,128]{1,0:T(8,128)(2,1)} %bitcast.3, s32[4]{0:T(128)} %len_ref.1, s32[256]{0:T(256)} %owner_ref.1, bf16[1024,5120]{1,0:T(8,128)(2,1)} %w_hbm.1), custom_call_target="tpu_custom_call" | custom-call | tf_op jit(solution)/shard_map/pallas_call | solution.py:491
  104.2 2.0 %copy.8 = bf16[512,640]{1,0:T(8,128)(2,1)} copy(bf16[512,640]{1,0:T(8,128)(2,1)} %shard_map.64) | data formatting | bytes 1310720

commit v7 on v6

--- a/solution.py
+++ b/solution.py
@@ -180,8 +180,7 @@
         def _():
             go(4, None, 1, sibling, part)
 
-    for part in range(2):
-        go(1, None, 8, far_x, part)
+    go(1, None, 8, far_x, 0)
 
     ends = []
     total = 0
@@ -222,6 +221,7 @@
         def _():
             arrived(4, 1)
             pass_block(4, 1)
+            go(1, None, 8, far_x, 1)
 
         c = i // 2
         pairs = (i % 2 * 2, i % 2 * 2 + 1)

time: 106 us -> 106 us (level)
  no operation moved by 1% of the time
where the time goes in v7:
time: 106 us
  Pallas kernels  104 us (98%)
  local copies, waits for them, and re-layouts  1.98 us (2%)
    pallas_call x1, Pallas kernels, attention(): pl.pallas_call(attend_kernel, out_shape=jax.ShapeDtypeStruct((ROWS, WIDTH...  104 us

profile of v7, /device:TPU:1, one launch (start us, length us, event | category | flops | bytes accessed | tf_op | source)
XLA Modules:
  0.0 106.0 jit_solution(11140219907375923943)
XLA Ops:
  0.0 104.0 %shard_map.64 = bf16[512,640]{1,0:T(8,128)(2,1)} custom-call(bf16[512,8,128]{2,1,0:T(8,128)(2,1)} %q_ref.1, bf16[512,128]{1,0:T(8,128)(2,1)} %bitcast.2, bf16[512,128]{1,0:T(8,128)(2,1)} %bitcast.3, s32[4]{0:T(128)} %len_ref.1, s32[256]{0:T(256)} %owner_ref.1, bf16[1024,5120]{1,0:T(8,128)(2,1)} %w_hbm.1), custom_call_target="tpu_custom_call" | custom-call | tf_op jit(solution)/shard_map/pallas_call | solution.py:491
  104.0 2.0 %copy.8 = bf16[512,640]{1,0:T(8,128)(2,1)} copy(bf16[512,640]{1,0:T(8,128)(2,1)} %shard_map.64) | data formatting | bytes 1310720
